TPU v7x, 32 devices: a whole 2x2x4 slice. The times are simulated.
32 devices in a mesh: row: 4 (over x, core), col: 8 (over z, y).
Axes of the slice: x: 2, y: 2, z: 4, core: 2. Of those that a mesh axis runs over, the one named last changes fastest.
Arguments:
- alignment: bfloat16 [32, 64, 256], P(None, ('row', 'col')), may hold values from -60 to 60
- norm_gain: float32 [256], replicated, may hold values from 0.1 to 1.9
- norm_bias: float32 [256], replicated, may hold values from -3 to 3
- proj_weight: bfloat16 [256, 64], replicated, may hold values from -0.375 to 0.375
- pair_weight: bfloat16 [1024, 128], replicated, may hold values from -1 to 1
- pair_bias: float32 [128], replicated, may hold values from -3 to 3
- head_weight: bfloat16 [128, 64], replicated, may hold values from -24 to 24
- head_bias: float32 [64], replicated, may hold values from -6 to 6
- labels: int32 [64, 64], P('row', 'col'), may hold values from 0 to 63, as said below
- pair_mask: int32 [64, 64], P('row', 'col'), may hold values from 0 to 1, as said below
- loss_scale: float32 [], replicated, may hold values from 256 to 1024
Outputs:
- distogram_loss: float32 [], replicated
- alignment_grad: float32 [32, 64, 256], P(None, ('row', 'col'))
- pair_weight_grad: float32 [1024, 128], replicated
Inputs may be any that keep to these rules, and one draw needn't show every extreme that they name: labels is symmetric, labels[i, i] = 0, and labels[0, 63] = labels[63, 0] = 63. pair_mask[i, j] = v[i] * v[j] for a 0/1 vector v over the residues, with v[0] = 1 and v[63] = 0.
All inputs are finite; a program needn't handle non-finite values.
Results may differ from a plain program's by a relative error of at most 0.0064.
Values may be sent and summed in bfloat16 or wider, within the bound.
No kernel may reach another device: no remote copies, remote signals or barrier semaphores. Data moves between devices by JAX's collectives and lax.ppermute only.
A program may use at most 64 MiB of HBM per device.

v0:
```python
import jax
import jax.numpy as jnp
from jax import lax
from jax.sharding import PartitionSpec as P

norm_eps = 1e-05
highest = lax.Precision.HIGHEST


def from_root(value, axis, source):
    kept = jnp.where(lax.axis_index(axis) == source, value, 0).astype(value.dtype)
    return lax.psum(kept, axis)


def normalize(alignment, norm_gain, norm_bias):
    values = alignment.astype(jnp.float32)
    centered = values - jnp.mean(values, axis=-1, keepdims=True)
    inverse = lax.rsqrt(jnp.mean(centered * centered, axis=-1, keepdims=True) + norm_eps)
    scaled = centered * inverse
    normed = (scaled * norm_gain + norm_bias).astype(jnp.bfloat16)
    return (scaled, inverse, normed)


def pair_features(left_proj, right_proj, mirrored):
    if mirrored:
        outer = jnp.einsum(
            "sid,sjc->ijcd", left_proj, right_proj, preferred_element_type=jnp.float32
        )
    else:
        outer = jnp.einsum(
            "sic,sjd->ijcd", left_proj, right_proj, preferred_element_type=jnp.float32
        )
    outer = outer * (1.0 / left_proj.shape[0])
    return outer.astype(jnp.bfloat16).reshape(-1, outer.shape[2] * outer.shape[3])


def local(
    alignment,
    norm_gain,
    norm_bias,
    proj_weight,
    pair_weight,
    pair_bias,
    head_weight,
    head_bias,
    labels,
    pair_mask,
    loss_scale,
):
    per_row = lax.axis_size("col") // lax.axis_size("row")
    col_place = lax.axis_index("col")
    row_place = lax.axis_index("row")
    sequences = alignment.shape[0]
    outer_width = proj_weight.shape[1] // 2
    bin_count = head_weight.shape[1]
    scaled, inverse, normed = normalize(alignment, norm_gain, norm_bias)
    projected = jnp.einsum(
        "src,cp->srp", normed, proj_weight, preferred_element_type=jnp.float32
    ).astype(jnp.bfloat16)
    mask_values = pair_mask.astype(jnp.float32)
    valid_pairs = lax.psum(jnp.sum(mask_values), ("row", "col"))
    row_proj = lax.all_gather(projected, "col", axis=1, tiled=True)
    row_span = row_proj.shape[1]
    col_span = row_span // per_row
    offset = col_place % per_row * col_span
    own_slice = lax.dynamic_slice_in_dim(row_proj, offset, col_span, 1)
    col_proj = from_root(own_slice, "row", col_place // per_row)
    pair32 = pair_weight.astype(jnp.float32)
    head32 = head_weight.astype(jnp.float32)
    weight_shape = pair32.shape
    grad_width = 2 * outer_width
    block_rows = min(row_span, max(1, 512 // col_span))
    num_blocks = row_span // block_rows
    grad_factor = loss_scale / valid_pairs
    inv_seqs = 1.0 / sequences
    bins_iota = lax.broadcasted_iota(jnp.int32, (block_rows * col_span, bin_count), 1)

    def pair_head(features):
        hidden = jnp.dot(features, pair_weight, preferred_element_type=jnp.float32) + pair_bias
        return jnp.dot(hidden, head32, precision=highest) + head_bias

    def tile_back(features, dhalf, left_proj, right_proj, mirrored):
        dhidden = jnp.dot(dhalf, head_weight.T, preferred_element_type=jnp.float32)
        dfeatures = jnp.dot(dhidden, pair32.T, precision=highest)
        weight_term = jnp.dot(features.astype(jnp.float32).T, dhidden, precision=highest)
        dfeatures = dfeatures.astype(jnp.bfloat16).reshape(
            left_proj.shape[1], right_proj.shape[1], outer_width, outer_width
        )
        if mirrored:
            grad_left = jnp.einsum(
                "ijcd,sjc->sid", dfeatures, right_proj, preferred_element_type=jnp.float32
            )
            grad_right = jnp.einsum(
                "ijcd,sid->sjc", dfeatures, left_proj, preferred_element_type=jnp.float32
            )
        else:
            grad_left = jnp.einsum(
                "ijcd,sjd->sic", dfeatures, right_proj, preferred_element_type=jnp.float32
            )
            grad_right = jnp.einsum(
                "ijcd,sic->sjd", dfeatures, left_proj, preferred_element_type=jnp.float32
            )
        return (grad_left * inv_seqs, grad_right * inv_seqs, weight_term)

    def block_step(block_index, carry):
        loss_sum, weight_sum, row_grad, col_grad = carry
        first_row = block_index * block_rows
        rows_here = lax.dynamic_slice_in_dim(row_proj, first_row, block_rows, 1)
        left_own = rows_here[:, :, :outer_width]
        left_mirror = rows_here[:, :, outer_width:]
        right_own = col_proj[:, :, outer_width:]
        right_mirror = col_proj[:, :, :outer_width]
        own_features = pair_features(left_own, right_own, False)
        mirror_features = pair_features(left_mirror, right_mirror, True)
        logits = pair_head(own_features) + pair_head(mirror_features)
        labels_here = lax.dynamic_slice_in_dim(labels, first_row, block_rows, 0).reshape(-1)
        mask_here = lax.dynamic_slice_in_dim(mask_values, first_row, block_rows, 0).reshape(-1)
        row_top = jnp.max(logits, axis=-1, keepdims=True)
        shifted = logits - row_top
        exp_shift = jnp.exp(shifted)
        exp_total = jnp.sum(exp_shift, axis=-1, keepdims=True)
        target = bins_iota == labels_here[:, None]
        picked = jnp.sum(jnp.where(target, shifted, 0.0), axis=-1)
        loss_sum = loss_sum + jnp.sum(mask_here * (jnp.log(exp_total[:, 0]) - picked))
        dlogits = (
            (exp_shift / exp_total - target.astype(jnp.float32))
            * (mask_here * grad_factor)[:, None]
        ).astype(jnp.bfloat16)
        grad_left, grad_right, weight_term = tile_back(
            own_features, dlogits, left_own, right_own, False
        )
        mirror_left, mirror_right, mirror_term = tile_back(
            mirror_features, dlogits, left_mirror, right_mirror, True
        )
        row_part = jnp.concatenate([grad_left, mirror_left], axis=-1)
        col_part = jnp.concatenate([mirror_right, grad_right], axis=-1)
        weight_term = weight_term + mirror_term
        row_grad = lax.dynamic_update_slice_in_dim(row_grad, row_part, first_row, 1)
        return (loss_sum, weight_sum + weight_term, row_grad, col_grad + col_part)

    initial = (
        jnp.zeros((), jnp.float32),
        jnp.zeros(weight_shape, jnp.float32),
        jnp.zeros((sequences, row_span, grad_width), jnp.float32),
        jnp.zeros((sequences, col_span, grad_width), jnp.float32),
    )
    loss_sum, weight_sum, row_grad, col_grad = lax.fori_loop(0, num_blocks, block_step, initial)
    holder = col_place // per_row == row_place
    col_sum = lax.psum(col_grad.astype(jnp.bfloat16), "row").astype(jnp.float32)
    placed = lax.dynamic_update_slice_in_dim(jnp.zeros_like(row_grad), col_sum, offset, 1)
    contribution = row_grad + jnp.where(holder, placed, 0.0)
    own_grad = lax.psum_scatter(contribution, "col", scatter_dimension=1, tiled=True)
    dnormed = jnp.einsum(
        "srp,cp->src", own_grad, proj_weight.astype(jnp.float32), precision=highest
    )
    dscaled = dnormed * norm_gain
    alignment_grad = inverse * (
        dscaled
        - jnp.mean(dscaled, axis=-1, keepdims=True)
        - scaled * jnp.mean(dscaled * scaled, axis=-1, keepdims=True)
    )
    loss_total, pair_weight_grad = lax.psum((loss_sum, weight_sum), ("row", "col"))
    return (loss_total / valid_pairs, alignment_grad, pair_weight_grad)


def solution(mesh):
    in_specs = (
        P(None, ("row", "col"), None),
        P(),
        P(),
        P(),
        P(),
        P(),
        P(),
        P(),
        P("row", "col"),
        P("row", "col"),
        P(),
    )
    out_specs = (P(), P(None, ("row", "col"), None), P())
    return jax.shard_map(local, mesh=mesh, in_specs=in_specs, out_specs=out_specs, check_vma=False)
```

profile of v0, /device:TPU:0, one launch (start us, length us, event | category | flops | bytes accessed | tf_op | source)
XLA Modules:
  0.0 263.7 jit_solution(3482542408303123230)
XLA Ops:
  8.0 0.0 copy-start
  8.0 0.0 reduce-scatter.2.cloned.1.call-start
  8.1 0.8 convert_reduce_fusion
  8.9 0.9 fusion.30
  9.9 1.0 convolution_convert_fusion.1
  10.9 32.3 %all_gather.3 = bf16[32,16,64]{2,0,1:T(8,128)(2,1)S(1)} all-gather(bf16[32,2,64]{2,0,1:T(8,128)(2,1)S(1)} %convolution_convert_fusion.1), channel_id=1, replica_groups=mesh['row'=4,'col'=8] {'col'}, dimensions={1}, use_global_device_ids=true | all-gather | bytes 73728 | tf_op jit(solution)/shard_map/all_gather | solution.py:62
  43.2 0.1 copy.49
  43.4 11.5 %psum.35 = bf16[32,8,64]{0,2,1:T(8,128)(2,1)S(1)} all-reduce(bf16[32,8,64]{0,2,1:T(8,128)(2,1)S(1)} %broadcast_select_fusion), channel_id=1, replica_groups=mesh['row'=4,'col'=8] {'row'}, use_global_device_ids=true, to_apply=%region_2.0 | all-reduce | flops 16384 | bytes 65536 | tf_op jit(solution)/shard_map/psum | solution.py:12
  54.9 0.4 fusion
  55.3 0.5 fusion.1
  56.4 0.1 copy.28
  56.5 0.1 copy.33
  56.6 0.6 eq.23
  57.2 0.6 copy.31
  57.8 1.1 reshape.61
  58.9 0.1 copy.32
  59.1 1.1 reshape.62
  60.2 0.2 convolution_add_fusion.2
  60.4 0.2 convolution_add_fusion.1
  60.7 0.2 convolution_add_fusion.4
  60.9 0.2 fusion.53
  61.1 0.1 sub.54
  61.2 0.6 convert_reduce_fusion.1
  61.8 40.4 %all-reduce = (f32[]{:T(128)}, f32[]{:T(128)}) all-reduce(f32[]{:T(128)} %get-tuple-element.53, f32[]{:T(128)} %get-tuple-element.52), channel_id=1, replica_groups=mesh['row'=4,'col'=8] {'row','col'}, use_global_device_ids=true, to_apply=%region_7.8 | all-reduce | flops 2 | bytes 16 | tf_op jit(solution)/shard_map/psum | solution.py:162
  102.9 0.1 mul.116
  103.0 0.2 fusion.47
  103.2 0.4 convolution_convert_fusion
  103.6 0.8 reshape.63
  104.4 0.9 fusion.6
  105.3 0.4 fusion.7
  105.7 0.3 fusion.3
  106.0 0.9 fusion.2
  106.9 0.1 pad_maximum_fusion.1
  107.1 10.7 %psum.38 = bf16[32,8,64]{2,0,1:T(8,128)(2,1)S(1)} all-reduce(bf16[32,8,64]{2,0,1:T(8,128)(2,1)S(1)} %pad_maximum_fusion.1), channel_id=1, replica_groups=mesh['row'=4,'col'=8] {'row'}, use_global_device_ids=true, to_apply=%region_10.11 | all-reduce | flops 16384 | bytes 65536 | tf_op jit(solution)/shard_map/psum | solution.py:149
  117.8 0.1 pad_maximum_fusion
  117.9 0.1 fusion.11
  118.0 0.7 copy-done.3
  118.7 0.0 reduce-scatter.2.cloned.1.call-update
  118.8 0.0 all-reduce.3.cloned.1.call-start
  118.8 0.4 fusion.54
  119.3 1.2 convolution_add_fusion
  120.5 0.0 all-reduce.3.cloned.1.call-update
  121.9 59.1 %reduce-scatter.2.cloned.1.call-done = f32[32,2,64]{2,0,1:T(8,128)} async-done(((f32[32,16,64]{2,0,1:T(8,128)}), f32[32,2,64]{2,0,1:T(8,128)}) %reduce-scatter.2.cloned.1.call-update) | async-done | bytes 16400 | tf_op jit(solution)/shard_map/reduce_scatter | solution.py:152
  181.0 1.0 fusion.52
  182.0 0.1 fusion.29
  182.1 0.7 copy.38
  182.8 70.5 %all-reduce.3.cloned.1.call-done = f32[1024,128]{1,0:T(8,128)} async-done(((f32[1024,128]{1,0:T(8,128)}), f32[1024,128]{1,0:T(8,128)}) %all-reduce.3.cloned.1.call-update) | async-done | bytes 524304 | tf_op jit(solution)/shard_map/psum | solution.py:162
  253.3 1.9 copy.61
  (32 shorter events, 0.2 us)
Async XLA Ops:
  8.0 52.2 %copy-start = (bf16[1024,128]{1,0:T(8,128)(2,1)S(1)}, bf16[1024,128]{1,0:T(8,128)(2,1)}, u32[]{:S(2)}) copy-start(bf16[1024,128]{1,0:T(8,128)(2,1)} %param.15) | copy-start | bytes 786436
  8.0 173.0 %reduce-scatter.2.cloned.1.call-start = ((), (), s32[]{:S(2)}) async-start(), calls=%async_computation.1 | async-start | bytes 294912 | tf_op jit(solution)/shard_map/reduce_scatter | solution.py:152
  54.8 0.9 copy-start.1
  54.9 1.6 copy-start.6
  54.9 1.7 copy-start.7
  59.0 1.1 copy-start.10
  59.0 1.6 copy-start.5
  59.1 1.6 copy-start.8
  60.2 0.9 copy-start.9
  104.4 1.3 copy-start.2
  118.0 0.7 copy-start.3
  118.8 134.5 %all-reduce.3.cloned.1.call-start = ((), (), s32[]{:S(2)}) async-start(), calls=%async_computation.2 | async-start | bytes 1048576 | tf_op jit(solution)/shard_map/psum | solution.py:162
  119.3 61.7 %copy-start.4 = (bf16[32,2,256]{2,1,0:T(2,128)(2,1)S(1)}, bf16[32,2,256]{2,1,0:T(2,128)(2,1)}, u32[]{:S(2)}) copy-start(bf16[32,2,256]{2,1,0:T(2,128)(2,1)} %param.11) | copy-start | bytes 98308
  119.3 61.7 %copy-start.11 = (bf16[256,64]{0,1:T(8,128)(2,1)S(1)}, bf16[256,64]{0,1:T(8,128)(2,1)}, u32[]{:S(2)}) copy-start(bf16[256,64]{0,1:T(8,128)(2,1)} %param.14) | copy-start | bytes 98308
  119.3 61.7 %copy-start.12 = (f32[256]{0:T(256)S(1)}, f32[256]{0:T(256)}, u32[]{:S(2)}) copy-start(f32[256]{0:T(256)} %param.12) | copy-start | bytes 3076
Sparse Core Ops, SparseCore 0:
  118.9 62.0 reduce-scatter.1
Sparse Core Ops, SparseCore 1:
  125.1 128.1 all-reduce.2
where the time goes:
time: 264 us
  waiting for transfers between devices  130 us (49%)
  blocking collectives  94.8 us (36%)
  between operations  19.7 us (7%)
  matrix products  8.53 us (3%)
  local copies, waits for them, and re-layouts  8.05 us (3%)
  other arithmetic  2.94 us (1%)
    psum x1, waiting for transfers between devices, local(): lax.psum((loss_sum, weight_sum), ('row', 'col'))  70.5 us
    reduce_scatter x1, waiting for transfers between devices, local(): lax.psum_scatter(contribution, 'col', scatter_dimension=1, tiled=True)  59.1 us
    psum x1, blocking collectives, local(): lax.psum((loss_sum, weight_sum), ('row', 'col'))  40.4 us
    all_gather x1, blocking collectives, local(): row_proj = lax.all_gather(projected, 'col', axis=1, tiled=True)  32.3 us
    psum x1, blocking collectives, from_root(): return lax.psum(kept, axis)  11.5 us
    psum x1, blocking collectives, local(): col_sum = lax.psum(col_grad.astype(jnp.bfloat16), 'row').astype(jnp.float32)  10.7 us
  transfers between devices with their start and end apart: 2, of which 2 were waited for; matrix products, arithmetic and copies ran while one was open for 1% of the time, Pallas kernels for 0%

commit v1 on v0

--- a/solution.py
+++ b/solution.py
@@ -1,6 +1,10 @@
+import functools
+
 import jax
 import jax.numpy as jnp
 from jax import lax
+from jax.experimental import pallas as pl
+from jax.experimental.pallas import tpu as pltpu
 from jax.sharding import PartitionSpec as P
 
 norm_eps = 1e-05
@@ -163,6 +167,252 @@
     return (loss_total / valid_pairs, alignment_grad, pair_weight_grad)
 
 
+f32 = jnp.float32
+bf16 = jnp.bfloat16
+NN = (((1,), (0,)), ((), ()))
+NT = (((1,), (1,)), ((), ()))
+
+
+def dot(a, b, dims=NN):
+    return lax.dot_general(a, b, dims, preferred_element_type=f32)
+
+
+def layer_norm(x):
+    centered = x - jnp.mean(x, axis=-1, keepdims=True)
+    inverse = lax.rsqrt(jnp.mean(centered * centered, axis=-1, keepdims=True) + norm_eps)
+    return centered * inverse, inverse
+
+
+def prepare_kernel(align_ref, gain_ref, bias_ref, weight_ref, labels_ref, mask_ref, out_ref):
+    align = align_ref[...].astype(f32)
+    weight = weight_ref[...]
+    plain = []
+    for r in range(2):
+        scaled, _ = layer_norm(align[:, r, :])
+        normed = (scaled * gain_ref[...] + bias_ref[...]).astype(bf16)
+        turned = dot(weight, normed, NT)
+        rows = [
+            jnp.concatenate([turned[h * 32 + q * 8 : h * 32 + q * 8 + 8] for q in range(4)], axis=1)
+            for h in range(2)
+        ]
+        out_ref[r * 16 : r * 16 + 16, :] = jnp.concatenate(rows, axis=0).astype(bf16)
+        plain.append(dot(normed, weight[32:64], NT))
+    out_ref[32:48, :] = jnp.concatenate(
+        [plain[r][h * 16 : h * 16 + 16] for h in range(2) for r in range(2)], axis=1
+    ).astype(bf16)
+    lane = lax.broadcasted_iota(jnp.int32, (16, 128), 1)
+    spread = (lane // 8 == lax.broadcasted_iota(jnp.int32, (16, 128), 0)).astype(bf16)
+    keep = lane[:8] % 8 == lax.broadcasted_iota(jnp.int32, (8, 128), 0)
+    flat = []
+    for ref in (labels_ref, mask_ref):
+        wide = dot(ref[...].astype(f32).astype(bf16), spread)
+        flat.append(jnp.sum(jnp.where(keep, wide, 0.0), axis=0, keepdims=True))
+    row = lax.broadcasted_iota(jnp.int32, (16, 128), 0)
+    out_ref[48:64, :] = jnp.where(row == 0, flat[0], jnp.where(row == 1, flat[1], 0.0)).astype(bf16)
+
+
+def pairs_kernel(
+    place_ref, scale_ref, gathered_ref, align_ref, gain_ref, proj_ref, pair_ref, pair_bias_ref,
+    head_ref, head_bias_ref, loss_ref, align_grad_ref, weight_grad_ref,
+    turned_ref, left_ref, wide_ref, pair_blocks_ref, pair32_ref, features_ref, hidden_ref, dhidden_ref,
+):
+    turned_ref[...] = gathered_ref[:, 0:32, :].reshape(1024, 128).astype(f32)
+    groups = [turned_ref[pl.ds(g, 64, stride=16), :].astype(bf16) for g in range(16)]
+    for g in range(8):
+        left_ref[g * 64 : g * 64 + 64, :] = groups[g]
+    source = lax.broadcasted_iota(jnp.int32, (128, 512), 0)
+    target = lax.broadcasted_iota(jnp.int32, (128, 512), 1)
+    copies = jnp.where(source == target // 128 * 32 + target % 32, 1.0 / 32.0, 0.0).astype(bf16)
+    wide_ref[...] = dot(gathered_ref[:, 32:48, :].reshape(512, 128), copies).astype(bf16)
+    for g in range(8):
+        for q in range(4):
+            at = (q * 8 + g) * 32
+            pair_blocks_ref[g * 128 + q * 32 : g * 128 + q * 32 + 32, :] = pair_ref[at : at + 32, :]
+    pair32_ref[...] = pair_ref[...].astype(f32)
+
+    lane = lax.broadcasted_iota(jnp.int32, (32, 128), 1) // 32
+
+    def forward(d, _):
+        top = pl.multiple_of(d * 16, 16)
+        sides = []
+        for r in range(2):
+            right = jnp.concatenate(
+                [wide_ref[pl.ds(top, 16), (h * 2 + r) * 128 : (h * 2 + r + 1) * 128] for h in range(2)], axis=0
+            )
+            sides.append(
+                jnp.concatenate([jnp.where(lane == q, right, jnp.zeros_like(right)) for q in range(4)], axis=0)
+            )
+        outer = dot(left_ref[...], jnp.concatenate(sides, axis=1)).astype(bf16)
+        first = pl.multiple_of(d * 128, 128)
+        features = jnp.concatenate(
+            [
+                jnp.concatenate([outer[g * 64 : g * 64 + 64, r * 128 : r * 128 + 128] for g in range(8)], axis=1)
+                for r in range(2)
+            ],
+            axis=0,
+        )
+        features_ref[pl.ds(first, 128), :] = features
+        hidden_ref[pl.ds(first, 128), :] = dot(features, pair_blocks_ref[...]) + pair_bias_ref[...]
+        return 0
+
+    lax.fori_loop(0, 32, forward, 0, unroll=2)
+
+    source = lax.broadcasted_iota(jnp.int32, (128, 1024), 0)
+    target = lax.broadcasted_iota(jnp.int32, (128, 1024), 1)
+    spread = (source == target // 64 * 8 + target % 8).astype(bf16)
+    keep = (
+        lax.broadcasted_iota(jnp.int32, (32, 1024), 1) // 8 % 8
+        == lax.broadcasted_iota(jnp.int32, (32, 1024), 0) % 8
+    )
+    turned_ref[0:512, :] = gathered_ref[:, 48:64, :].reshape(512, 128).astype(f32)
+
+    def blocks(row):
+        placed = dot(turned_ref[pl.ds(row, 32, stride=16), :].astype(bf16), spread)
+        return jnp.sum(jnp.where(keep, placed, 0.0).reshape(4, 8, 1024), axis=1)
+
+    labels = blocks(0).astype(jnp.int32)
+    mask = blocks(1)
+    valid = jnp.sum(mask, keepdims=True)
+    factor = mask * (scale_ref[0] / valid)
+    head_t = head_ref[...]
+    head_twice = jnp.concatenate([head_t, head_t], axis=1)
+    head2 = (2.0 * head_t.astype(f32).T).astype(bf16)
+    head_bias2 = 2.0 * head_bias_ref[...]
+    bins = lax.broadcasted_iota(jnp.int32, (64, 256), 0)
+    loss = jnp.zeros((1, 256), f32)
+    for k in range(16):
+        both = jnp.concatenate(
+            [
+                hidden_ref[j * 64 : j * 64 + 64, :] + hidden_ref[pl.ds(j, 64, stride=64), :]
+                for j in range(k * 4, k * 4 + 4)
+            ],
+            axis=0,
+        )
+        high = both.astype(bf16)
+        low = (both - high.astype(f32)).astype(bf16)
+        logits = dot(head_twice, jnp.concatenate([high, low], axis=1), NT) + head_bias2
+        part = slice(k % 4 * 256, k % 4 * 256 + 256)
+        labels_here = labels[k // 4 : k // 4 + 1, part]
+        shifted = logits - jnp.max(logits, axis=0, keepdims=True)
+        exp_shift = jnp.exp(shifted)
+        exp_total = jnp.sum(exp_shift, axis=0, keepdims=True)
+        hit = bins == labels_here
+        picked = jnp.sum(jnp.where(hit, shifted, 0.0), axis=0, keepdims=True)
+        loss = loss + mask[k // 4 : k // 4 + 1, part] * (jnp.log(exp_total) - picked)
+        dlogits = (exp_shift / exp_total - jnp.where(hit, 1.0, 0.0)) * factor[k // 4 : k // 4 + 1, part]
+        dhidden_ref[:, k * 256 : k * 256 + 256] = dot(head2, dlogits.astype(bf16)).astype(bf16)
+    loss_ref[...] = jnp.sum(loss, axis=1, keepdims=True) / valid
+
+    for n in range(4):
+        turned = dot(dhidden_ref[...], features_ref[:, n * 256 : n * 256 + 256]).T
+        for g in range(2):
+            for q in range(4):
+                at = (q * 8 + n * 2 + g) * 32
+                weight_grad_ref[at : at + 32, :] = turned[g * 128 + q * 32 : g * 128 + q * 32 + 32]
+
+    place = place_ref[0]
+    own = dhidden_ref[:, pl.ds(pl.multiple_of(place * 128, 128), 128)]
+    own = jnp.concatenate([own[:, 0:64], own[:, 64:128]], axis=0)
+    sums = dot(own, jnp.concatenate(groups, axis=1)).astype(bf16)
+
+    def contract(weights, base):
+        q_rows = jnp.concatenate(
+            [
+                jnp.concatenate(
+                    [sums[r * 128 : r * 128 + 128, (base + g) * 128 : (base + g + 1) * 128] for r in range(2)], axis=1
+                )
+                for g in range(8)
+            ],
+            axis=0,
+        )
+        full = dot(jnp.concatenate(weights, axis=1), q_rows)
+        row = lax.broadcasted_iota(jnp.int32, (128, 256), 0) // 32
+        col = lax.broadcasted_iota(jnp.int32, (128, 256), 1) // 32 % 4
+        kept = jnp.where(row == col, full, 0.0)
+        return kept[0:32] + kept[32:64] + kept[64:96] + kept[96:128]
+
+    by_left = [pair_blocks_ref[g * 128 : g * 128 + 128, :] for g in range(8)]
+    by_right = [
+        jnp.concatenate([pair32_ref[pl.ds(q * 8 + g, 32, stride=32), :] for q in range(4)], axis=0).astype(bf16)
+        for g in range(8)
+    ]
+    dleft = contract(by_right, 8)
+    dright = contract(by_left, 0)
+    dproj = jnp.concatenate([dleft, dright], axis=0).T * (1.0 / 32.0)
+    proj = proj_ref[...]
+    proj_twice = jnp.concatenate([proj, proj], axis=0)
+    align = align_ref[...].astype(f32)
+    for r in range(2):
+        at = r * 128
+        one = dproj[at : at + 32] + dproj[at + 32 : at + 64] + dproj[at + 64 : at + 96] + dproj[at + 96 : at + 128]
+        high = one.astype(bf16)
+        low = (one - high.astype(f32)).astype(bf16)
+        dscaled = dot(jnp.concatenate([high, low], axis=1), proj_twice) * gain_ref[...]
+        scaled, inverse = layer_norm(align[:, r, :])
+        align_grad_ref[:, r, :] = inverse * (
+            dscaled
+            - jnp.mean(dscaled, axis=-1, keepdims=True)
+            - scaled * jnp.mean(dscaled * scaled, axis=-1, keepdims=True)
+        )
+
+
+def spec(space=pltpu.VMEM):
+    return pl.BlockSpec(memory_space=space)
+
+
+def prepare(align, gain, bias, proj_t, labels_t, mask_t):
+    return pl.pallas_call(
+        prepare_kernel,
+        out_shape=jax.ShapeDtypeStruct((64, 128), bf16),
+        in_specs=[spec()] * 6,
+        out_specs=spec(),
+    )(align, gain, bias, proj_t, labels_t, mask_t)
+
+
+def pairs(place, scale, gathered, align, gain, proj_t, pair, pair_bias, head_t, head_bias):
+    return pl.pallas_call(
+        pairs_kernel,
+        out_shape=(
+            jax.ShapeDtypeStruct((1, 1), f32),
+            jax.ShapeDtypeStruct((32, 2, 256), f32),
+            jax.ShapeDtypeStruct((1024, 128), f32),
+        ),
+        in_specs=[spec(pltpu.SMEM)] * 2 + [spec()] * 8,
+        out_specs=(spec(),) * 3,
+        scratch_shapes=[
+            pltpu.VMEM((1024, 128), f32),
+            pltpu.VMEM((512, 128), bf16),
+            pltpu.VMEM((512, 512), bf16),
+            pltpu.VMEM((1024, 128), bf16),
+            pltpu.VMEM((1024, 128), f32),
+            pltpu.VMEM((4096, 1024), bf16),
+            pltpu.VMEM((4096, 128), f32),
+            pltpu.VMEM((128, 4096), bf16),
+        ],
+        compiler_params=pltpu.CompilerParams(vmem_limit_bytes=40 * 1024 * 1024),
+    )(place, scale, gathered, align, gain, proj_t, pair, pair_bias, head_t, head_bias)
+
+
+def gather(message):
+    copies = jnp.broadcast_to(message[None], (32,) + message.shape)
+    return lax.all_to_all(copies, ("row", "col"), 0, 0, tiled=True)
+
+
+def local_whole(
+    alignment, norm_gain, norm_bias, proj_weight, pair_weight, pair_bias, head_weight, head_bias,
+    labels, pair_mask, loss_scale,
+):
+    gain = norm_gain.reshape(1, 256)
+    message = prepare(alignment, gain, norm_bias.reshape(1, 256), proj_weight.T, labels.T, pair_mask.T)
+    gathered = gather(message)
+    place = lax.axis_index(("row", "col")).astype(jnp.int32).reshape(1)
+    loss, align_grad, weight_grad = pairs(
+        place, loss_scale.reshape(1), gathered, alignment, gain, proj_weight.T, pair_weight,
+        pair_bias.reshape(1, 128), head_weight.T, head_bias.reshape(64, 1),
+    )
+    return (loss.reshape(()), align_grad, weight_grad)
+
+
 def solution(mesh):
     in_specs = (
         P(None, ("row", "col"), None),
@@ -178,4 +428,17 @@
         P(),
     )
     out_specs = (P(), P(None, ("row", "col"), None), P())
-    return jax.shard_map(local, mesh=mesh, in_specs=in_specs, out_specs=out_specs, check_vma=False)
+    def whole(alignment, *others):
+        sequences, residues, channels = alignment.shape
+        small = (
+            (sequences, residues, channels) == (32, 64, 256)
+            and tuple(mesh.shape.values()) == (4, 8)
+            and others[2].shape[1] == 64
+            and others[3].shape == (1024, 128)
+            and others[5].shape == (128, 64)
+        )
+        return jax.shard_map(
+            local_whole if small else local, mesh=mesh, in_specs=in_specs, out_specs=out_specs, check_vma=False
+        )(alignment, *others)
+
+    return whole

time: 264 us -> 45.4 us (0.17)
  waiting for transfers between devices: 130 us -> 15.6 us
  blocking collectives: 94.8 us -> 0 us
  Pallas kernels: 0 us -> 18.4 us
  between operations: 19.7 us -> 1.35 us
  matrix products: 8.53 us -> 0 us
  starting transfers between devices: 0.08 us -> 7.3 us
  local copies, waits for them, and re-layouts: 8.05 us -> 2.4 us
  other arithmetic: 2.94 us -> 0 us
    psum x1 -> x0, waiting for transfers between devices: 70.5 us -> none  [local(): lax.psum((loss_sum, weight_sum), ('row', 'col'))]
    psum x3 -> x0, blocking collectives: 62.5 us -> none  [the longest x1 40.4 us: local(): lax.psum((loss_sum, weight_sum), ('row', 'col'))]
    reduce_scatter x1 -> x0, waiting for transfers between devices: 59.1 us -> none  [local(): lax.psum_scatter(contribution, 'col', scatter_dimension=1, tiled=True)]
    all_gather x1 -> x0, blocking collectives: 32.3 us -> none  [local(): row_proj = lax.all_gather(projected, 'col', axis=1, tiled=True)]
    pallas_call x0 -> x2, Pallas kernels: none -> 18.4 us  [the longest x1 16.6 us: pairs(): pl.pallas_call(pairs_kernel, out_shape=(jax.ShapeDtypeStruct((1, 1), f32)...]
    all_to_all x0 -> x1, waiting for transfers between devices: none -> 15.6 us  [gather(): return lax.all_to_all(copies, ('row', 'col'), 0, 0, tiled=True)]
    dot_general x16 -> x0, matrix products: 8.53 us -> none  [the longest x2 1.67 us: tile_back(): jnp.dot(features.astype(jnp.float32).T, dhidden, precision=highest)]
    all_to_all x0 -> x1, starting transfers between devices: none -> 7.3 us  [gather(): return lax.all_to_all(copies, ('row', 'col'), 0, 0, tiled=True)]
  transfers between devices with their start and end apart: 2 -> 1, of which waited for: 2 -> 1; matrix products, arithmetic and copies ran while one was open for 1% -> 0% of each run, Pallas kernels for 0% -> 0%
where the time goes in v1:
time: 45.4 us; the launch traced here: 45 us
  Pallas kernels  18.4 us (41%)
  waiting for transfers between devices  15.6 us (34%)
  starting transfers between devices  7.3 us (16%)
  local copies, waits for them, and re-layouts  2.4 us (5%)
  between operations  1.35 us (3%)
    pallas_call x1, Pallas kernels, pairs(): pl.pallas_call(pairs_kernel, out_shape=(jax.ShapeDtypeStruct((1, 1), f32)...  16.6 us
    all_to_all x1, waiting for transfers between devices, gather(): return lax.all_to_all(copies, ('row', 'col'), 0, 0, tiled=True)  15.6 us
    all_to_all x1, starting transfers between devices, gather(): return lax.all_to_all(copies, ('row', 'col'), 0, 0, tiled=True)  7.3 us
    pallas_call x1, Pallas kernels, prepare(): pl.pallas_call(prepare_kernel, out_shape=jax.ShapeDtypeStruct((64, 128),...  1.82 us
    broadcast_in_dim x1, local copies, waits for them, and re-layouts, gather(): copies = jnp.broadcast_to(message[None], (32,) + message.shape)  1.63 us
  transfers between devices with their start and end apart: 1, of which 1 were waited for; matrix products, arithmetic and copies ran while one was open for 0% of the time, Pallas kernels for 0%

profile of v1, /device:TPU:0, one launch (start us, length us, event | category | flops | bytes accessed | tf_op | source)
XLA Modules:
  0.0 45.0 jit_solution(1564762221897825570)
XLA Ops:
  0.6 1.8 %shard_map.130 = bf16[64,128]{1,0:T(8,128)(2,1)} custom-call(bf16[32,2,256]{2,1,0:T(2,128)(2,1)} %align_ref.3, f32[1,256]{1,0:T(1,128)} %bitcast.15, f32[1,256]{1,0:T(1,128)} %bitcast.20, bf16[64,256]{1,0:T(8,128)(2,1)} %bitcast.12, s32[8,16]{1,0:T(8,128)} %bitcast.18, s32[8,16]{1,0:T(8,128)} %bitcast.19), custom_call_target="tpu_custom_call" | custom-call | tf_op jit(solution)/shard_map/pallas_call | solution.py:364
  2.4 1.6 %broadcast_in_dim.2 = bf16[32,64,128]{2,1,0:T(8,128)(2,1)} broadcast(bf16[64,128]{1,0:T(8,128)(2,1)} %shard_map.130), dimensions={1,2} | broadcast | bytes 540672 | tf_op jit(solution)/shard_map/broadcast_in_dim | solution.py:397
  4.1 0.0 copy-start.6
  4.1 0.0 copy-start
  4.1 0.0 copy-start.2
  4.1 7.3 %all-to-all-start = ((bf16[32,64,128]{2,1,0:T(8,128)(2,1)}), bf16[32,64,128]{2,1,0:T(8,128)(2,1)S(1)}, u32[]{:S(2)}, u32[]{:S(2)}) async-start(bf16[32,64,128]{2,1,0:T(8,128)(2,1)} %broadcast_in_dim.2), calls=%async_computation | async-start | bytes 1048576 | tf_op jit(solution)/shard_map/all_to_all | solution.py:398
  11.4 0.0 copy-start.1
  12.1 0.0 copy-done.6
  12.1 0.0 copy-start.3
  12.1 0.1 copy.14.head_bias_ref
  12.2 15.6 %all-to-all-done.gathered_ref = bf16[32,64,128]{2,1,0:T(8,128)(2,1)S(1)} async-done(((bf16[32,64,128]{2,1,0:T(8,128)(2,1)}), bf16[32,64,128]{2,1,0:T(8,128)(2,1)S(1)}, u32[]{:S(2)}, u32[]{:S(2)}) %all-to-all-start) | async-done | bytes 524320 | tf_op jit(solution)/shard_map/all_to_all | solution.py:398
  27.7 0.0 copy-start.4
  27.7 0.0 copy-start.5
  27.7 0.0 copy-done
  27.7 0.0 copy-done.2
  27.8 0.0 copy-done.1
  27.8 0.0 copy-done.3
  27.8 0.6 %copy-done.4 = f32[256]{0:T(256)S(1)} copy-done((f32[256]{0:T(256)S(1)}, f32[256]{0:T(256)}, u32[]{:S(2)}) %copy-start.4) | copy-done | bytes 1048
  28.4 0.0 copy-done.5
  28.4 16.6 %shard_map.131 = (f32[1,1]{1,0:T(1,128)}, f32[32,2,256]{2,1,0:T(2,128)}, f32[1024,128]{1,0:T(8,128)}) custom-call(s32[1]{0:T(128)} %bitcast.place_ref, f32[1]{0:T(128)} %bitcast.11.scale_ref, bf16[32,64,128]{2,1,0:T(8,128)(2,1)S(1)} %all-to-all-done.gathered_ref, bf16[32,2,256]{2,1,0:T(2,128)(2,1)S(1)} %copy-done.1, f32[1,256]{1,0:T(1,128)S(1)} %bitcast.16, ...), custom_call_target="tpu_custom_call" | custom-call | tf_op jit(solution)/shard_map/pallas_call | solution.py:373
Async XLA Ops:
  4.1 8.0 %copy-start.6 = (f32[64]{0:T(128)S(1)}, f32[64]{0:T(128)}, u32[]{:S(2)}) copy-start(f32[64]{0:T(128)} %param.18) | copy-start | bytes 772
  4.1 23.7 %copy-start = (bf16[1024,128]{1,0:T(8,128)(2,1)S(1)}, bf16[1024,128]{1,0:T(8,128)(2,1)}, u32[]{:S(2)}) copy-start(bf16[1024,128]{1,0:T(8,128)(2,1)} %pair_ref.1) | copy-start | bytes 786436
  4.1 23.7 %copy-start.2 = (bf16[256,64]{0,1:T(8,128)(2,1)S(1)}, bf16[256,64]{0,1:T(8,128)(2,1)}, u32[]{:S(2)}) copy-start(bf16[256,64]{0,1:T(8,128)(2,1)} %param.14) | copy-start | bytes 98308
  4.1 23.7 %all-to-all-start = ((bf16[32,64,128]{2,1,0:T(8,128)(2,1)}), bf16[32,64,128]{2,1,0:T(8,128)(2,1)S(1)}, u32[]{:S(2)}, u32[]{:S(2)}) async-start(bf16[32,64,128]{2,1,0:T(8,128)(2,1)} %broadcast_in_dim.2), calls=%async_computation | async-start | bytes 1048576 | tf_op jit(solution)/shard_map/all_to_all | solution.py:398
  11.4 16.4 %copy-start.1 = (bf16[32,2,256]{2,1,0:T(2,128)(2,1)S(1)}, bf16[32,2,256]{2,1,0:T(2,128)(2,1)}, u32[]{:S(2)}) copy-start(bf16[32,2,256]{2,1,0:T(2,128)(2,1)} %align_ref.3) | copy-start | bytes 98308
  12.1 15.7 %copy-start.3 = (bf16[128,64]{0,1:T(8,128)(2,1)S(1)}, bf16[128,64]{0,1:T(8,128)(2,1)}, u32[]{:S(2)}) copy-start(bf16[128,64]{0,1:T(8,128)(2,1)} %param.17) | copy-start | bytes 49156
  27.7 0.7 %copy-start.4 = (f32[256]{0:T(256)S(1)}, f32[256]{0:T(256)}, u32[]{:S(2)}) copy-start(f32[256]{0:T(256)} %param.12) | copy-start | bytes 3076
  27.7 0.7 %copy-start.5 = (f32[128]{0:T(128)S(1)}, f32[128]{0:T(128)}, u32[]{:S(2)}) copy-start(f32[128]{0:T(128)} %param.16) | copy-start | bytes 1540

commit v2 on v1

--- a/solution.py
+++ b/solution.py
@@ -183,7 +183,21 @@
     return centered * inverse, inverse
 
 
-def prepare_kernel(align_ref, gain_ref, bias_ref, weight_ref, labels_ref, mask_ref, out_ref):
+def fetch(sources, targets, sems):
+    copies = [
+        pltpu.make_async_copy(source, target, sems.at[n])
+        for n, (source, target) in enumerate(zip(sources, targets, strict=True))
+    ]
+    for copy in copies:
+        copy.start()
+    return copies
+
+
+def prepare_kernel(*refs):
+    out_ref = refs[6]
+    for copy in fetch(refs[:6], refs[7:13], refs[13]):
+        copy.wait()
+    align_ref, gain_ref, bias_ref, weight_ref, labels_ref, mask_ref = refs[7:13]
     align = align_ref[...].astype(f32)
     weight = weight_ref[...]
     plain = []
@@ -211,25 +225,58 @@
     out_ref[48:64, :] = jnp.where(row == 0, flat[0], jnp.where(row == 1, flat[1], 0.0)).astype(bf16)
 
 
+def arrange_weights(pair_ref, pair_bias, head_t, head_bias, folded_ref, by_left_ref, by_right_ref, pair32_ref):
+    pair32_ref[...] = pair_ref[...].astype(f32)
+    head_twice = jnp.concatenate([head_t, head_t], axis=0)
+    lane = lax.broadcasted_iota(jnp.int32, (128, 128), 1)
+    for g in range(8):
+        for q in range(4):
+            at = (q * 8 + g) * 32
+            by_left_ref[q * 32 : q * 32 + 32, g * 128 : g * 128 + 128] = pair_ref[at : at + 32, :]
+            by_right_ref[q * 32 : q * 32 + 32, g * 128 : g * 128 + 128] = pair32_ref[
+                pl.ds(q * 8 + g, 32, stride=32), :
+            ].astype(bf16)
+        product = dot(by_left_ref[:, g * 128 : g * 128 + 128], head_twice, NT)
+        high = product.astype(bf16).astype(f32)
+        folded_ref[g * 128 : g * 128 + 128, :] = jnp.where(lane < 64, high, product - high).astype(bf16)
+    row = lax.broadcasted_iota(jnp.int32, (64, 64), 0)
+    col = lax.broadcasted_iota(jnp.int32, (64, 64), 1)
+    own_bias = jnp.sum(jnp.where(row == col, head_bias, 0.0), axis=1, keepdims=True)
+    return 2.0 * (jnp.sum(head_t.astype(f32) * pair_bias, axis=1, keepdims=True) + own_bias)
+
+
 def pairs_kernel(
-    place_ref, scale_ref, gathered_ref, align_ref, gain_ref, proj_ref, pair_ref, pair_bias_ref,
-    head_ref, head_bias_ref, loss_ref, align_grad_ref, weight_grad_ref,
-    turned_ref, left_ref, wide_ref, pair_blocks_ref, pair32_ref, features_ref, hidden_ref, dhidden_ref,
+    place_ref, scale_ref, *refs
 ):
-    turned_ref[...] = gathered_ref[:, 0:32, :].reshape(1024, 128).astype(f32)
+    pieces, sources, refs = refs[:8], refs[8:15], refs[15:]
+    (
+        loss_ref, align_grad_ref, weight_grad_ref,
+        turned_ref, left_ref, plain_ref, wide_ref, flat_ref, features_ref, half_ref, dhidden_ref,
+        folded_ref, by_left_ref, by_right_ref, pair32_ref,
+        pair_ref, pair_bias_ref, head_ref, head_bias_ref, align_ref, gain_ref, proj_ref, sems,
+    ) = refs
+    transfers = fetch(sources, refs[15:22], sems)
+    place = place_ref[0]
+    for n, piece in enumerate(pieces):
+        for k in range(4):
+            sender = place ^ (n // 4 * 8 + n // 2 % 2 * 16 + n % 2 + k * 2)
+            at = k * 64
+            turned_ref[pl.ds(pl.multiple_of(sender * 32, 32), 32), :] = piece[at : at + 32, :].astype(f32)
+            plain_ref[pl.ds(pl.multiple_of(sender * 16, 16), 16), :] = piece[at + 32 : at + 48, :]
+            flat_ref[pl.ds(pl.multiple_of(sender * 16, 16), 16), :] = piece[at + 48 : at + 64, :].astype(f32)
     groups = [turned_ref[pl.ds(g, 64, stride=16), :].astype(bf16) for g in range(16)]
     for g in range(8):
         left_ref[g * 64 : g * 64 + 64, :] = groups[g]
     source = lax.broadcasted_iota(jnp.int32, (128, 512), 0)
     target = lax.broadcasted_iota(jnp.int32, (128, 512), 1)
     copies = jnp.where(source == target // 128 * 32 + target % 32, 1.0 / 32.0, 0.0).astype(bf16)
-    wide_ref[...] = dot(gathered_ref[:, 32:48, :].reshape(512, 128), copies).astype(bf16)
-    for g in range(8):
-        for q in range(4):
-            at = (q * 8 + g) * 32
-            pair_blocks_ref[g * 128 + q * 32 : g * 128 + q * 32 + 32, :] = pair_ref[at : at + 32, :]
-    pair32_ref[...] = pair_ref[...].astype(f32)
-
+    wide_ref[...] = dot(plain_ref[...], copies).astype(bf16)
+
+    for transfer in transfers:
+        transfer.wait()
+    bias = arrange_weights(
+        pair_ref, pair_bias_ref[...], head_ref[...], head_bias_ref[...], folded_ref, by_left_ref, by_right_ref, pair32_ref
+    )
     lane = lax.broadcasted_iota(jnp.int32, (32, 128), 1) // 32
 
     def forward(d, _):
@@ -252,10 +299,10 @@
             axis=0,
         )
         features_ref[pl.ds(first, 128), :] = features
-        hidden_ref[pl.ds(first, 128), :] = dot(features, pair_blocks_ref[...]) + pair_bias_ref[...]
+        half_ref[pl.ds(first, 128), :] = dot(features, folded_ref[...])
         return 0
 
-    lax.fori_loop(0, 32, forward, 0, unroll=2)
+    lax.fori_loop(0, 32, forward, 0, unroll=32)
 
     source = lax.broadcasted_iota(jnp.int32, (128, 1024), 0)
     target = lax.broadcasted_iota(jnp.int32, (128, 1024), 1)
@@ -264,33 +311,29 @@
         lax.broadcasted_iota(jnp.int32, (32, 1024), 1) // 8 % 8
         == lax.broadcasted_iota(jnp.int32, (32, 1024), 0) % 8
     )
-    turned_ref[0:512, :] = gathered_ref[:, 48:64, :].reshape(512, 128).astype(f32)
 
     def blocks(row):
-        placed = dot(turned_ref[pl.ds(row, 32, stride=16), :].astype(bf16), spread)
+        placed = dot(flat_ref[pl.ds(row, 32, stride=16), :].astype(bf16), spread)
         return jnp.sum(jnp.where(keep, placed, 0.0).reshape(4, 8, 1024), axis=1)
 
     labels = blocks(0).astype(jnp.int32)
     mask = blocks(1)
     valid = jnp.sum(mask, keepdims=True)
     factor = mask * (scale_ref[0] / valid)
-    head_t = head_ref[...]
-    head_twice = jnp.concatenate([head_t, head_t], axis=1)
-    head2 = (2.0 * head_t.astype(f32).T).astype(bf16)
-    head_bias2 = 2.0 * head_bias_ref[...]
+    head2 = (2.0 * head_ref[...].astype(f32).T).astype(bf16)
     bins = lax.broadcasted_iota(jnp.int32, (64, 256), 0)
     loss = jnp.zeros((1, 256), f32)
     for k in range(16):
-        both = jnp.concatenate(
-            [
-                hidden_ref[j * 64 : j * 64 + 64, :] + hidden_ref[pl.ds(j, 64, stride=64), :]
-                for j in range(k * 4, k * 4 + 4)
-            ],
-            axis=0,
-        )
-        high = both.astype(bf16)
-        low = (both - high.astype(f32)).astype(bf16)
-        logits = dot(head_twice, jnp.concatenate([high, low], axis=1), NT) + head_bias2
+        sums = []
+        for p in range(2):
+            at = k * 256 + p * 128
+            j = k * 4 + p * 2
+            mirrored = jnp.concatenate(
+                [half_ref[pl.ds(j, 64, stride=64), :], half_ref[pl.ds(j + 1, 64, stride=64), :]], axis=0
+            )
+            both = (half_ref[at : at + 128, :] + mirrored).T
+            sums.append(both[0:64] + both[64:128])
+        logits = jnp.concatenate(sums, axis=1) + bias
         part = slice(k % 4 * 256, k % 4 * 256 + 256)
         labels_here = labels[k // 4 : k // 4 + 1, part]
         shifted = logits - jnp.max(logits, axis=0, keepdims=True)
@@ -310,7 +353,6 @@
                 at = (q * 8 + n * 2 + g) * 32
                 weight_grad_ref[at : at + 32, :] = turned[g * 128 + q * 32 : g * 128 + q * 32 + 32]
 
-    place = place_ref[0]
     own = dhidden_ref[:, pl.ds(pl.multiple_of(place * 128, 128), 128)]
     own = jnp.concatenate([own[:, 0:64], own[:, 64:128]], axis=0)
     sums = dot(own, jnp.concatenate(groups, axis=1)).astype(bf16)
@@ -325,19 +367,14 @@
             ],
             axis=0,
         )
-        full = dot(jnp.concatenate(weights, axis=1), q_rows)
+        full = dot(weights, q_rows)
         row = lax.broadcasted_iota(jnp.int32, (128, 256), 0) // 32
         col = lax.broadcasted_iota(jnp.int32, (128, 256), 1) // 32 % 4
         kept = jnp.where(row == col, full, 0.0)
         return kept[0:32] + kept[32:64] + kept[64:96] + kept[96:128]
 
-    by_left = [pair_blocks_ref[g * 128 : g * 128 + 128, :] for g in range(8)]
-    by_right = [
-        jnp.concatenate([pair32_ref[pl.ds(q * 8 + g, 32, stride=32), :] for q in range(4)], axis=0).astype(bf16)
-        for g in range(8)
-    ]
-    dleft = contract(by_right, 8)
-    dright = contract(by_left, 0)
+    dleft = contract(by_right_ref[...], 8)
+    dright = contract(by_left_ref[...], 0)
     dproj = jnp.concatenate([dleft, dright], axis=0).T * (1.0 / 32.0)
     proj = proj_ref[...]
     proj_twice = jnp.concatenate([proj, proj], axis=0)
@@ -360,16 +397,30 @@
     return pl.BlockSpec(memory_space=space)
 
 
+def far(*arrays):
+    return [pltpu.with_memory_space_constraint(a, pltpu.HBM) for a in arrays]
+
+
+def held(*arrays):
+    return [pltpu.VMEM(a.shape, a.dtype) for a in arrays] + [pltpu.SemaphoreType.DMA((len(arrays),))]
+
+
+def limit(mib):
+    return pltpu.CompilerParams(vmem_limit_bytes=mib * 1024 * 1024)
+
+
 def prepare(align, gain, bias, proj_t, labels_t, mask_t):
     return pl.pallas_call(
         prepare_kernel,
         out_shape=jax.ShapeDtypeStruct((64, 128), bf16),
-        in_specs=[spec()] * 6,
+        in_specs=[spec(pltpu.HBM)] * 6,
         out_specs=spec(),
-    )(align, gain, bias, proj_t, labels_t, mask_t)
-
-
-def pairs(place, scale, gathered, align, gain, proj_t, pair, pair_bias, head_t, head_bias):
+        scratch_shapes=held(align, gain, bias, proj_t, labels_t, mask_t),
+        compiler_params=limit(2),
+    )(*far(align, gain, bias, proj_t, labels_t, mask_t))
+
+
+def pairs(place, scale, pieces, *others):
     return pl.pallas_call(
         pairs_kernel,
         out_shape=(
@@ -377,25 +428,50 @@
             jax.ShapeDtypeStruct((32, 2, 256), f32),
             jax.ShapeDtypeStruct((1024, 128), f32),
         ),
-        in_specs=[spec(pltpu.SMEM)] * 2 + [spec()] * 8,
+        in_specs=[spec(pltpu.SMEM)] * 2 + [spec()] * 8 + [spec(pltpu.HBM)] * 7,
         out_specs=(spec(),) * 3,
         scratch_shapes=[
             pltpu.VMEM((1024, 128), f32),
             pltpu.VMEM((512, 128), bf16),
+            pltpu.VMEM((512, 128), bf16),
             pltpu.VMEM((512, 512), bf16),
-            pltpu.VMEM((1024, 128), bf16),
-            pltpu.VMEM((1024, 128), f32),
+            pltpu.VMEM((512, 128), f32),
             pltpu.VMEM((4096, 1024), bf16),
             pltpu.VMEM((4096, 128), f32),
             pltpu.VMEM((128, 4096), bf16),
-        ],
-        compiler_params=pltpu.CompilerParams(vmem_limit_bytes=40 * 1024 * 1024),
-    )(place, scale, gathered, align, gain, proj_t, pair, pair_bias, head_t, head_bias)
+            pltpu.VMEM((1024, 128), bf16),
+            pltpu.VMEM((128, 1024), bf16),
+            pltpu.VMEM((128, 1024), bf16),
+            pltpu.VMEM((1024, 128), f32),
+        ]
+        + held(*others),
+        compiler_params=limit(24),
+    )(place, scale, *pieces, *far(*others))
+
+
+def join_kernel(*refs):
+    for n, part in enumerate(refs[:4]):
+        refs[4][n * 64 : n * 64 + 64, :] = part[...]
+
+
+def join(parts):
+    return pl.pallas_call(
+        join_kernel,
+        out_shape=jax.ShapeDtypeStruct((256, 128), bf16),
+        in_specs=[spec()] * 4,
+        out_specs=spec(),
+        compiler_params=limit(2),
+    )(*parts)
 
 
 def gather(message):
-    copies = jnp.broadcast_to(message[None], (32,) + message.shape)
-    return lax.all_to_all(copies, ("row", "col"), 0, 0, tiled=True)
+    def swap(block, row_bits, col_bits):
+        moves = [(d, (d // 8 ^ row_bits) * 8 + (d % 8 ^ col_bits)) for d in range(32)]
+        return lax.ppermute(block, ("row", "col"), moves)
+
+    line = join([message] + [swap(message, 0, 2 * k) for k in range(1, 4)])
+    plane = [line] + [swap(line, n // 2 * 2, n % 2) for n in range(1, 4)]
+    return plane + [swap(block, 1, 0) for block in plane]
 
 
 def local_whole(
@@ -404,11 +480,11 @@
 ):
     gain = norm_gain.reshape(1, 256)
     message = prepare(alignment, gain, norm_bias.reshape(1, 256), proj_weight.T, labels.T, pair_mask.T)
-    gathered = gather(message)
+    pieces = gather(message)
     place = lax.axis_index(("row", "col")).astype(jnp.int32).reshape(1)
     loss, align_grad, weight_grad = pairs(
-        place, loss_scale.reshape(1), gathered, alignment, gain, proj_weight.T, pair_weight,
-        pair_bias.reshape(1, 128), head_weight.T, head_bias.reshape(64, 1),
+        place, loss_scale.reshape(1), pieces, pair_weight, pair_bias.reshape(1, 128), head_weight.T,
+        head_bias.reshape(1, 64), alignment, gain, proj_weight.T,
     )
     return (loss.reshape(()), align_grad, weight_grad)
 

time: 45.4 us -> 31.5 us (0.69)
  waiting for transfers between devices: 15.6 us -> 8.33 us
  Pallas kernels: 18.4 us -> 12.3 us
  local copies, waits for them, and re-layouts: 2.4 us -> 0 us
  starting transfers between devices: 7.3 us -> 9.32 us
    all_to_all x1 -> x0, waiting for transfers between devices: 15.6 us -> none  [gather(): return lax.all_to_all(copies, ('row', 'col'), 0, 0, tiled=True)]
    ppermute x0 -> x10, starting transfers between devices: none -> 9.32 us  [swap(): return lax.ppermute(block, ('row', 'col'), moves)]
    ppermute x0 -> x10, waiting for transfers between devices: none -> 8.33 us  [swap(): return lax.ppermute(block, ('row', 'col'), moves)]
    all_to_all x1 -> x0, starting transfers between devices: 7.3 us -> none  [gather(): return lax.all_to_all(copies, ('row', 'col'), 0, 0, tiled=True)]
    pallas_call x1, Pallas kernels: 16.6 us -> 11 us  [pairs(): pl.pallas_call(pairs_kernel, out_shape=(jax.ShapeDtypeStruct((1, 1), f32)...]
    broadcast_in_dim x1 -> x0, local copies, waits for them, and re-layouts: 1.63 us -> none  [gather(): copies = jnp.broadcast_to(message[None], (32,) + message.shape)]
    unnamed x14 -> x0, local copies, waits for them, and re-layouts: 0.68 us -> none
    pallas_call x1, Pallas kernels: 1.82 us -> 1.28 us  [prepare(): pl.pallas_call(prepare_kernel, out_shape=jax.ShapeDtypeStruct((64, 128),...]
  transfers between devices with their start and end apart: 1 -> 10, of which waited for: 1 -> 6; matrix products, arithmetic and copies ran while one was open for 0% -> 0% of each run, Pallas kernels for 0% -> 0%
where the time goes in v2:
time: 31.5 us; the launch traced here: 31.2 us
  Pallas kernels  12.3 us (39%)
  starting transfers between devices  9.32 us (30%)
  waiting for transfers between devices  8.33 us (26%)
  between operations  1.32 us (4%)
    pallas_call x1, Pallas kernels, pairs(): pl.pallas_call(pairs_kernel, out_shape=(jax.ShapeDtypeStruct((1, 1), f32)...  11 us
    ppermute x10, starting transfers between devices, swap(): return lax.ppermute(block, ('row', 'col'), moves)  9.32 us
    ppermute x10, waiting for transfers between devices, swap(): return lax.ppermute(block, ('row', 'col'), moves)  8.33 us
    pallas_call x1, Pallas kernels, prepare(): pl.pallas_call(prepare_kernel, out_shape=jax.ShapeDtypeStruct((64, 128),...  1.28 us
  transfers between devices with their start and end apart: 10, of which 6 were waited for; matrix products, arithmetic and copies ran while one was open for 0% of the time, Pallas kernels for 0%

profile of v2, /device:TPU:0, one launch (start us, length us, event | category | flops | bytes accessed | tf_op | source)
XLA Modules:
  0.0 31.2 jit_solution(13200296979377539828)
XLA Ops:
  0.6 1.3 %shard_map.130.refs_0_ = bf16[64,128]{1,0:T(8,128)(2,1)S(1)} custom-call(bf16[32,2,256]{2,1,0:T(2,128)(2,1)} %refs_12_.1, f32[1,256]{1,0:T(1,128)} %bitcast.15, f32[1,256]{1,0:T(1,128)} %bitcast.19, bf16[64,256]{1,0:T(8,128)(2,1)} %bitcast.12, s32[8,16]{1,0:T(8,128)} %bitcast.17, s32[8,16]{1,0:T(8,128)} %bitcast.18), custom_call_target="tpu_custom_call" | custom-call | tf_op jit(solution)/shard_map/pallas_call | solution.py:413
  1.9 5.1 %collective-permute-start.2 = (bf16[64,128]{1,0:T(8,128)(2,1)S(1)}, bf16[64,128]{1,0:T(8,128)(2,1)S(1)}, u32[]{:S(2)}, u32[]{:S(2)}) collective-permute-start(bf16[64,128]{1,0:T(8,128)(2,1)S(1)} %shard_map.130.refs_0_), channel_id=1, source_target_pairs={{0,6},{1,7},{2,4},{3,5},{4,2},{5,3},{6,0},{7,1},{8,14},{9,15},{10,... | collective-permute-start | bytes 49160 | tf_op jit(solution)/shard_map/ppermute | solution.py:470
  7.0 0.0 collective-permute-start.1
  7.0 0.6 %collective-permute-start = (bf16[64,128]{1,0:T(8,128)(2,1)S(1)}, bf16[64,128]{1,0:T(8,128)(2,1)S(1)}, u32[]{:S(2)}, u32[]{:S(2)}) collective-permute-start(bf16[64,128]{1,0:T(8,128)(2,1)S(1)} %shard_map.130.refs_0_), channel_id=1, source_target_pairs={{0,2},{1,3},{2,0},{3,1},{4,6},{5,7},{6,4},{7,5},{8,10},{9,11},{10,... | collective-permute-start | bytes 49160 | tf_op jit(solution)/shard_map/ppermute | solution.py:470
  7.7 1.1 %collective-permute-done.2.refs_3_ = bf16[64,128]{1,0:T(8,128)(2,1)S(1)} collective-permute-done((bf16[64,128]{1,0:T(8,128)(2,1)S(1)}, bf16[64,128]{1,0:T(8,128)(2,1)S(1)}, u32[]{:S(2)}, u32[]{:S(2)}) %collective-permute-start.2) | collective-permute-done | bytes 16416 | tf_op jit(solution)/shard_map/ppermute | solution.py:470
  8.8 2.9 %collective-permute-done.1.refs_2_ = bf16[64,128]{1,0:T(8,128)(2,1)S(1)} collective-permute-done((bf16[64,128]{1,0:T(8,128)(2,1)S(1)}, bf16[64,128]{1,0:T(8,128)(2,1)S(1)}, u32[]{:S(2)}, u32[]{:S(2)}) %collective-permute-start.1) | collective-permute-done | bytes 16416 | tf_op jit(solution)/shard_map/ppermute | solution.py:470
  11.7 0.0 collective-permute-done.refs_1_
  11.7 2.5 %collective-permute-start.5 = (bf16[256,128]{1,0:T(8,128)(2,1)S(1)}, bf16[256,128]{1,0:T(8,128)(2,1)S(1)}, u32[]{:S(2)}, u32[]{:S(2)}) collective-permute-start(bf16[256,128]{1,0:T(8,128)(2,1)S(1)} %shard_map.131.refs_0_), channel_id=1, source_target_pairs={{0,17},{1,16},{2,19},{3,18},{4,21},{5,20},{6,23},{7,22},{8,25},{9,... | collective-permute-start | bytes 196616 | tf_op jit(solution)/shard_map/ppermute | solution.py:470
  14.2 0.5 %collective-permute-start.4 = (bf16[256,128]{1,0:T(8,128)(2,1)S(1)}, bf16[256,128]{1,0:T(8,128)(2,1)S(1)}, u32[]{:S(2)}, u32[]{:S(2)}) collective-permute-start(bf16[256,128]{1,0:T(8,128)(2,1)S(1)} %shard_map.131.refs_0_), channel_id=1, source_target_pairs={{0,16},{1,17},{2,18},{3,19},{4,20},{5,21},{6,22},{7,23},{8,24},{9,... | collective-permute-start | bytes 196616 | tf_op jit(solution)/shard_map/ppermute | solution.py:470
  14.7 0.5 %collective-permute-start.3 = (bf16[256,128]{1,0:T(8,128)(2,1)S(1)}, bf16[256,128]{1,0:T(8,128)(2,1)S(1)}, u32[]{:S(2)}, u32[]{:S(2)}) collective-permute-start(bf16[256,128]{1,0:T(8,128)(2,1)S(1)} %shard_map.131.refs_0_), channel_id=1, source_target_pairs={{0,1},{1,0},{2,3},{3,2},{4,5},{5,4},{6,7},{7,6},{8,9},{9,8},{10,11... | collective-permute-start | bytes 196616 | tf_op jit(solution)/shard_map/ppermute | solution.py:470
  15.2 0.0 collective-permute-start.6
  15.2 1.7 %collective-permute-done.5.refs_3_ = bf16[256,128]{1,0:T(8,128)(2,1)S(1)} collective-permute-done((bf16[256,128]{1,0:T(8,128)(2,1)S(1)}, bf16[256,128]{1,0:T(8,128)(2,1)S(1)}, u32[]{:S(2)}, u32[]{:S(2)}) %collective-permute-start.5) | collective-permute-done | bytes 65568 | tf_op jit(solution)/shard_map/ppermute | solution.py:470
  16.9 0.0 collective-permute-start.9
  16.9 1.5 %collective-permute-done.4.refs_2_ = bf16[256,128]{1,0:T(8,128)(2,1)S(1)} collective-permute-done((bf16[256,128]{1,0:T(8,128)(2,1)S(1)}, bf16[256,128]{1,0:T(8,128)(2,1)S(1)}, u32[]{:S(2)}, u32[]{:S(2)}) %collective-permute-start.4) | collective-permute-done | bytes 65568 | tf_op jit(solution)/shard_map/ppermute | solution.py:470
  18.5 0.0 collective-permute-start.8
  18.5 0.5 %collective-permute-done.3.refs_1_ = bf16[256,128]{1,0:T(8,128)(2,1)S(1)} collective-permute-done((bf16[256,128]{1,0:T(8,128)(2,1)S(1)}, bf16[256,128]{1,0:T(8,128)(2,1)S(1)}, u32[]{:S(2)}, u32[]{:S(2)}) %collective-permute-start.3) | collective-permute-done | bytes 65568 | tf_op jit(solution)/shard_map/ppermute | solution.py:470
  19.0 0.0 collective-permute-start.7
  19.7 0.0 collective-permute-done.6.refs_4_
  19.7 0.0 collective-permute-done.9.refs_7_
  19.7 0.0 collective-permute-done.8.refs_6_
  19.7 0.5 %collective-permute-done.7.refs_5_ = bf16[256,128]{1,0:T(8,128)(2,1)S(1)} collective-permute-done((bf16[256,128]{1,0:T(8,128)(2,1)S(1)}, bf16[256,128]{1,0:T(8,128)(2,1)S(1)}, u32[]{:S(2)}, u32[]{:S(2)}) %collective-permute-start.7) | collective-permute-done | bytes 65568 | tf_op jit(solution)/shard_map/ppermute | solution.py:470
  20.3 11.0 %shard_map.132 = (f32[1,1]{1,0:T(1,128)}, f32[32,2,256]{2,1,0:T(2,128)}, f32[1024,128]{1,0:T(8,128)}) custom-call(s32[1]{0:T(128)} %bitcast.place_ref, f32[1]{0:T(128)} %bitcast.11.scale_ref, bf16[256,128]{1,0:T(8,128)(2,1)S(1)} %shard_map.131.refs_0_, bf16[256,128]{1,0:T(8,128)(2,1)S(1)} %collective-permute-done.3.refs_1_, ...), custom_call_target="tpu_custom_call" | custom-call | tf_op jit(solution)/shard_map/pallas_call | solution.py:424
  (1 shorter events, 0.0 us)
Async XLA Ops:
  1.9 6.8 %collective-permute-start.2 = (bf16[64,128]{1,0:T(8,128)(2,1)S(1)}, bf16[64,128]{1,0:T(8,128)(2,1)S(1)}, u32[]{:S(2)}, u32[]{:S(2)}) collective-permute-start(bf16[64,128]{1,0:T(8,128)(2,1)S(1)} %shard_map.130.refs_0_), channel_id=1, source_target_pairs={{0,6},{1,7},{2,4},{3,5},{4,2},{5,3},{6,0},{7,1},{8,14},{9,15},{10,... | collective-permute-start | bytes 49160 | tf_op jit(solution)/shard_map/ppermute | solution.py:470
  7.0 4.6 %collective-permute-start.1 = (bf16[64,128]{1,0:T(8,128)(2,1)S(1)}, bf16[64,128]{1,0:T(8,128)(2,1)S(1)}, u32[]{:S(2)}, u32[]{:S(2)}) collective-permute-start(bf16[64,128]{1,0:T(8,128)(2,1)S(1)} %shard_map.130.refs_0_), channel_id=1, source_target_pairs={{0,4},{1,5},{2,6},{3,7},{4,0},{5,1},{6,2},{7,3},{8,12},{9,13},{10,... | collective-permute-start | bytes 49160 | tf_op jit(solution)/shard_map/ppermute | solution.py:470
  7.0 4.6 %collective-permute-start = (bf16[64,128]{1,0:T(8,128)(2,1)S(1)}, bf16[64,128]{1,0:T(8,128)(2,1)S(1)}, u32[]{:S(2)}, u32[]{:S(2)}) collective-permute-start(bf16[64,128]{1,0:T(8,128)(2,1)S(1)} %shard_map.130.refs_0_), channel_id=1, source_target_pairs={{0,2},{1,3},{2,0},{3,1},{4,6},{5,7},{6,4},{7,5},{8,10},{9,11},{10,... | collective-permute-start | bytes 49160 | tf_op jit(solution)/shard_map/ppermute | solution.py:470
  11.7 5.2 %collective-permute-start.5 = (bf16[256,128]{1,0:T(8,128)(2,1)S(1)}, bf16[256,128]{1,0:T(8,128)(2,1)S(1)}, u32[]{:S(2)}, u32[]{:S(2)}) collective-permute-start(bf16[256,128]{1,0:T(8,128)(2,1)S(1)} %shard_map.131.refs_0_), channel_id=1, source_target_pairs={{0,17},{1,16},{2,19},{3,18},{4,21},{5,20},{6,23},{7,22},{8,25},{9,... | collective-permute-start | bytes 196616 | tf_op jit(solution)/shard_map/ppermute | solution.py:470
  14.2 4.3 %collective-permute-start.4 = (bf16[256,128]{1,0:T(8,128)(2,1)S(1)}, bf16[256,128]{1,0:T(8,128)(2,1)S(1)}, u32[]{:S(2)}, u32[]{:S(2)}) collective-permute-start(bf16[256,128]{1,0:T(8,128)(2,1)S(1)} %shard_map.131.refs_0_), channel_id=1, source_target_pairs={{0,16},{1,17},{2,18},{3,19},{4,20},{5,21},{6,22},{7,23},{8,24},{9,... | collective-permute-start | bytes 196616 | tf_op jit(solution)/shard_map/ppermute | solution.py:470
  14.7 4.3 %collective-permute-start.3 = (bf16[256,128]{1,0:T(8,128)(2,1)S(1)}, bf16[256,128]{1,0:T(8,128)(2,1)S(1)}, u32[]{:S(2)}, u32[]{:S(2)}) collective-permute-start(bf16[256,128]{1,0:T(8,128)(2,1)S(1)} %shard_map.131.refs_0_), channel_id=1, source_target_pairs={{0,1},{1,0},{2,3},{3,2},{4,5},{5,4},{6,7},{7,6},{8,9},{9,8},{10,11... | collective-permute-start | bytes 196616 | tf_op jit(solution)/shard_map/ppermute | solution.py:470
  15.2 4.4 %collective-permute-start.6 = (bf16[256,128]{1,0:T(8,128)(2,1)S(1)}, bf16[256,128]{1,0:T(8,128)(2,1)S(1)}, u32[]{:S(2)}, u32[]{:S(2)}) collective-permute-start(bf16[256,128]{1,0:T(8,128)(2,1)S(1)} %shard_map.131.refs_0_), channel_id=1, source_target_pairs={{0,8},{1,9},{2,10},{3,11},{4,12},{5,13},{6,14},{7,15},{8,0},{9,1},... | collective-permute-start | bytes 196616 | tf_op jit(solution)/shard_map/ppermute | solution.py:470
  16.9 2.8 %collective-permute-start.9 = (bf16[256,128]{1,0:T(8,128)(2,1)S(1)}, bf16[256,128]{1,0:T(8,128)(2,1)S(1)}, u32[]{:S(2)}, u32[]{:S(2)}) collective-permute-start(bf16[256,128]{1,0:T(8,128)(2,1)S(1)} %collective-permute-done.5.refs_3_), channel_id=1, source_target_pairs={{0,8},{1,9},{2,10},{3,11},{4,12},{5,13},{6,14},{7,15},{8,0},{9,1},... | collective-permute-start | bytes 196616 | tf_op jit(solution)/shard_map/ppermute | solution.py:470
  18.5 1.3 %collective-permute-start.8 = (bf16[256,128]{1,0:T(8,128)(2,1)S(1)}, bf16[256,128]{1,0:T(8,128)(2,1)S(1)}, u32[]{:S(2)}, u32[]{:S(2)}) collective-permute-start(bf16[256,128]{1,0:T(8,128)(2,1)S(1)} %collective-permute-done.4.refs_2_), channel_id=1, source_target_pairs={{0,8},{1,9},{2,10},{3,11},{4,12},{5,13},{6,14},{7,15},{8,0},{9,1},... | collective-permute-start | bytes 196616 | tf_op jit(solution)/shard_map/ppermute | solution.py:470
  19.0 1.3 %collective-permute-start.7 = (bf16[256,128]{1,0:T(8,128)(2,1)S(1)}, bf16[256,128]{1,0:T(8,128)(2,1)S(1)}, u32[]{:S(2)}, u32[]{:S(2)}) collective-permute-start(bf16[256,128]{1,0:T(8,128)(2,1)S(1)} %collective-permute-done.3.refs_1_), channel_id=1, source_target_pairs={{0,8},{1,9},{2,10},{3,11},{4,12},{5,13},{6,14},{7,15},{8,0},{9,1},... | collective-permute-start | bytes 196616 | tf_op jit(solution)/shard_map/ppermute | solution.py:470

commit v3 on v2

--- a/solution.py
+++ b/solution.py
@@ -194,10 +194,12 @@
 
 
 def prepare_kernel(*refs):
-    out_ref = refs[6]
-    for copy in fetch(refs[:6], refs[7:13], refs[13]):
+    sources, out_ref, near, scratch, sems = refs[:10], refs[10], refs[11:18], refs[18:21], refs[21]
+    align_ref, gain_ref, weight_ref = near[:3]
+    bias_ref, labels_ref, mask_ref = scratch
+    copies = fetch(sources, near[:3] + scratch + near[3:], sems)
+    for copy in copies[:6]:
         copy.wait()
-    align_ref, gain_ref, bias_ref, weight_ref, labels_ref, mask_ref = refs[7:13]
     align = align_ref[...].astype(f32)
     weight = weight_ref[...]
     plain = []
@@ -223,9 +225,14 @@
         flat.append(jnp.sum(jnp.where(keep, wide, 0.0), axis=0, keepdims=True))
     row = lax.broadcasted_iota(jnp.int32, (16, 128), 0)
     out_ref[48:64, :] = jnp.where(row == 0, flat[0], jnp.where(row == 1, flat[1], 0.0)).astype(bf16)
-
-
-def arrange_weights(pair_ref, pair_bias, head_t, head_bias, folded_ref, by_left_ref, by_right_ref, pair32_ref):
+    for copy in copies[6:]:
+        copy.wait()
+
+
+def weights_kernel(
+    pair_ref, pair_bias_ref, head_ref, head_bias_ref, folded_ref, by_left_ref, by_right_ref, bias_ref, pair32_ref
+):
+    head_t = head_ref[...]
     pair32_ref[...] = pair_ref[...].astype(f32)
     head_twice = jnp.concatenate([head_t, head_t], axis=0)
     lane = lax.broadcasted_iota(jnp.int32, (128, 128), 1)
@@ -241,21 +248,19 @@
         folded_ref[g * 128 : g * 128 + 128, :] = jnp.where(lane < 64, high, product - high).astype(bf16)
     row = lax.broadcasted_iota(jnp.int32, (64, 64), 0)
     col = lax.broadcasted_iota(jnp.int32, (64, 64), 1)
-    own_bias = jnp.sum(jnp.where(row == col, head_bias, 0.0), axis=1, keepdims=True)
-    return 2.0 * (jnp.sum(head_t.astype(f32) * pair_bias, axis=1, keepdims=True) + own_bias)
+    own_bias = jnp.sum(jnp.where(row == col, head_bias_ref[...], 0.0), axis=1, keepdims=True)
+    bias_ref[...] = 2.0 * (jnp.sum(head_t.astype(f32) * pair_bias_ref[...], axis=1, keepdims=True) + own_bias)
 
 
 def pairs_kernel(
     place_ref, scale_ref, *refs
 ):
-    pieces, sources, refs = refs[:8], refs[8:15], refs[15:]
+    pieces, refs = refs[:8], refs[8:]
     (
+        folded_ref, by_left_ref, by_right_ref, bias_ref, head_ref, align_ref, gain_ref, proj_ref,
         loss_ref, align_grad_ref, weight_grad_ref,
         turned_ref, left_ref, plain_ref, wide_ref, flat_ref, features_ref, half_ref, dhidden_ref,
-        folded_ref, by_left_ref, by_right_ref, pair32_ref,
-        pair_ref, pair_bias_ref, head_ref, head_bias_ref, align_ref, gain_ref, proj_ref, sems,
     ) = refs
-    transfers = fetch(sources, refs[15:22], sems)
     place = place_ref[0]
     for n, piece in enumerate(pieces):
         for k in range(4):
@@ -264,7 +269,10 @@
             turned_ref[pl.ds(pl.multiple_of(sender * 32, 32), 32), :] = piece[at : at + 32, :].astype(f32)
             plain_ref[pl.ds(pl.multiple_of(sender * 16, 16), 16), :] = piece[at + 32 : at + 48, :]
             flat_ref[pl.ds(pl.multiple_of(sender * 16, 16), 16), :] = piece[at + 48 : at + 64, :].astype(f32)
-    groups = [turned_ref[pl.ds(g, 64, stride=16), :].astype(bf16) for g in range(16)]
+    groups = [
+        jnp.concatenate([turned_ref[pl.ds(p * 16 + g, 32, stride=32), :] for p in range(2)], axis=0).astype(bf16)
+        for g in range(16)
+    ]
     for g in range(8):
         left_ref[g * 64 : g * 64 + 64, :] = groups[g]
     source = lax.broadcasted_iota(jnp.int32, (128, 512), 0)
@@ -272,45 +280,49 @@
     copies = jnp.where(source == target // 128 * 32 + target % 32, 1.0 / 32.0, 0.0).astype(bf16)
     wide_ref[...] = dot(plain_ref[...], copies).astype(bf16)
 
-    for transfer in transfers:
-        transfer.wait()
-    bias = arrange_weights(
-        pair_ref, pair_bias_ref[...], head_ref[...], head_bias_ref[...], folded_ref, by_left_ref, by_right_ref, pair32_ref
-    )
     lane = lax.broadcasted_iota(jnp.int32, (32, 128), 1) // 32
 
-    def forward(d, _):
-        top = pl.multiple_of(d * 16, 16)
+    def outer_products(d):
         sides = []
         for r in range(2):
             right = jnp.concatenate(
-                [wide_ref[pl.ds(top, 16), (h * 2 + r) * 128 : (h * 2 + r + 1) * 128] for h in range(2)], axis=0
+                [wide_ref[d * 16 : d * 16 + 16, (h * 2 + r) * 128 : (h * 2 + r + 1) * 128] for h in range(2)], axis=0
             )
             sides.append(
                 jnp.concatenate([jnp.where(lane == q, right, jnp.zeros_like(right)) for q in range(4)], axis=0)
             )
         outer = dot(left_ref[...], jnp.concatenate(sides, axis=1)).astype(bf16)
-        first = pl.multiple_of(d * 128, 128)
-        features = jnp.concatenate(
-            [
-                jnp.concatenate([outer[g * 64 : g * 64 + 64, r * 128 : r * 128 + 128] for g in range(8)], axis=1)
-                for r in range(2)
-            ],
-            axis=0,
-        )
-        features_ref[pl.ds(first, 128), :] = features
-        half_ref[pl.ds(first, 128), :] = dot(features, folded_ref[...])
-        return 0
-
-    lax.fori_loop(0, 32, forward, 0, unroll=32)
+        for r in range(2):
+            for p in range(2):
+                at = d // 2 * 256 + (p + r) % 2 * 128 + d % 2 * 64 + r * 32
+                for g in range(8):
+                    features_ref[at : at + 32, g * 128 : g * 128 + 128] = outer[
+                        g * 64 + p * 32 : g * 64 + p * 32 + 32, r * 128 : r * 128 + 128
+                    ]
+
+    side = lax.broadcasted_iota(jnp.int32, (128, 128), 1) < 64
+
+    def half_logits(d):
+        at = d // 2 * 256 + d % 2 * 64
+        rows = jnp.concatenate([features_ref[at + h : at + h + 64, :] for h in (0, 128)], axis=0)
+        part = dot(rows, folded_ref[...])
+        part = part + pltpu.roll(part, 64, 1)
+        half_ref[d * 64 : d * 64 + 64, :] = jnp.where(side[0:64], part[0:64], part[64:128])
+
+    early = 2
+    for d in range(early):
+        outer_products(d)
+    for d in range(32):
+        if d + early < 32:
+            outer_products(d + early)
+        half_logits(d)
 
     source = lax.broadcasted_iota(jnp.int32, (128, 1024), 0)
     target = lax.broadcasted_iota(jnp.int32, (128, 1024), 1)
-    spread = (source == target // 64 * 8 + target % 8).astype(bf16)
-    keep = (
-        lax.broadcasted_iota(jnp.int32, (32, 1024), 1) // 8 % 8
-        == lax.broadcasted_iota(jnp.int32, (32, 1024), 0) % 8
-    )
+    first = target // 256 * 4 + target // 32 % 4
+    second = target % 32 * 2 + (target // 128 + first) % 2
+    spread = (source == first * 8 + second % 8).astype(bf16)
+    keep = second[0:32] // 8 == lax.broadcasted_iota(jnp.int32, (32, 1024), 0) % 8
 
     def blocks(row):
         placed = dot(flat_ref[pl.ds(row, 32, stride=16), :].astype(bf16), spread)
@@ -324,16 +336,13 @@
     bins = lax.broadcasted_iota(jnp.int32, (64, 256), 0)
     loss = jnp.zeros((1, 256), f32)
     for k in range(16):
-        sums = []
-        for p in range(2):
-            at = k * 256 + p * 128
-            j = k * 4 + p * 2
-            mirrored = jnp.concatenate(
-                [half_ref[pl.ds(j, 64, stride=64), :], half_ref[pl.ds(j + 1, 64, stride=64), :]], axis=0
-            )
-            both = (half_ref[at : at + 128, :] + mirrored).T
-            sums.append(both[0:64] + both[64:128])
-        logits = jnp.concatenate(sums, axis=1) + bias
+        rows = []
+        for j in (k * 2, k * 2 + 1):
+            even = half_ref[pl.ds(j, 32, stride=64), :]
+            odd = half_ref[pl.ds(j + 32, 32, stride=64), :]
+            rows += [jnp.where(side[0:32], even, odd), jnp.where(side[0:32], odd, even)]
+        both = (half_ref[k * 128 : k * 128 + 128, :] + jnp.concatenate(rows, axis=0)).T
+        logits = jnp.concatenate([both[0:64], both[64:128]], axis=1) + bias_ref[...]
         part = slice(k % 4 * 256, k % 4 * 256 + 256)
         labels_here = labels[k // 4 : k // 4 + 1, part]
         shifted = logits - jnp.max(logits, axis=0, keepdims=True)
@@ -342,7 +351,8 @@
         hit = bins == labels_here
         picked = jnp.sum(jnp.where(hit, shifted, 0.0), axis=0, keepdims=True)
         loss = loss + mask[k // 4 : k // 4 + 1, part] * (jnp.log(exp_total) - picked)
-        dlogits = (exp_shift / exp_total - jnp.where(hit, 1.0, 0.0)) * factor[k // 4 : k // 4 + 1, part]
+        here = factor[k // 4 : k // 4 + 1, part]
+        dlogits = exp_shift * (here / exp_total) - jnp.where(hit, here, 0.0)
         dhidden_ref[:, k * 256 : k * 256 + 256] = dot(head2, dlogits.astype(bf16)).astype(bf16)
     loss_ref[...] = jnp.sum(loss, axis=1, keepdims=True) / valid
 
@@ -353,8 +363,15 @@
                 at = (q * 8 + n * 2 + g) * 32
                 weight_grad_ref[at : at + 32, :] = turned[g * 128 + q * 32 : g * 128 + q * 32 + 32]
 
-    own = dhidden_ref[:, pl.ds(pl.multiple_of(place * 128, 128), 128)]
-    own = jnp.concatenate([own[:, 0:64], own[:, 64:128]], axis=0)
+    own = dhidden_ref[:, pl.ds(pl.multiple_of(place // 2 * 256, 256), 256)]
+    own = [jnp.where(place % 2 == 0, own[:, n : n + 64], own[:, n + 64 : n + 128]) for n in (0, 128)]
+    own = jnp.concatenate(
+        [
+            jnp.concatenate([own[0][:, 0:32], own[1][:, 0:32]], axis=1),
+            jnp.concatenate([own[1][:, 32:64], own[0][:, 32:64]], axis=1),
+        ],
+        axis=0,
+    )
     sums = dot(own, jnp.concatenate(groups, axis=1)).astype(bf16)
 
     def contract(weights, base):
@@ -402,22 +419,40 @@
 
 
 def held(*arrays):
-    return [pltpu.VMEM(a.shape, a.dtype) for a in arrays] + [pltpu.SemaphoreType.DMA((len(arrays),))]
+    return [pltpu.VMEM(a.shape, a.dtype) for a in arrays]
 
 
 def limit(mib):
     return pltpu.CompilerParams(vmem_limit_bytes=mib * 1024 * 1024)
 
 
-def prepare(align, gain, bias, proj_t, labels_t, mask_t):
+def prepare(align, gain, proj_t, bias, labels_t, mask_t, *others):
+    near = (align, gain, proj_t) + others
+    local = (bias, labels_t, mask_t)
     return pl.pallas_call(
         prepare_kernel,
-        out_shape=jax.ShapeDtypeStruct((64, 128), bf16),
-        in_specs=[spec(pltpu.HBM)] * 6,
-        out_specs=spec(),
-        scratch_shapes=held(align, gain, bias, proj_t, labels_t, mask_t),
+        out_shape=[jax.ShapeDtypeStruct((64, 128), bf16)] + [jax.ShapeDtypeStruct(a.shape, a.dtype) for a in near],
+        in_specs=[spec(pltpu.HBM)] * 10,
+        out_specs=[spec()] * 8,
+        scratch_shapes=held(*local) + [pltpu.SemaphoreType.DMA((10,))],
         compiler_params=limit(2),
-    )(*far(align, gain, bias, proj_t, labels_t, mask_t))
+    )(*far(*near[:3], *local, *others))
+
+
+def weights(*operands):
+    return pl.pallas_call(
+        weights_kernel,
+        out_shape=(
+            jax.ShapeDtypeStruct((1024, 128), bf16),
+            jax.ShapeDtypeStruct((128, 1024), bf16),
+            jax.ShapeDtypeStruct((128, 1024), bf16),
+            jax.ShapeDtypeStruct((64, 1), f32),
+        ),
+        in_specs=[spec()] * 4,
+        out_specs=[spec()] * 4,
+        scratch_shapes=[pltpu.VMEM((1024, 128), f32)],
+        compiler_params=limit(4),
+    )(*operands)
 
 
 def pairs(place, scale, pieces, *others):
@@ -428,7 +463,7 @@
             jax.ShapeDtypeStruct((32, 2, 256), f32),
             jax.ShapeDtypeStruct((1024, 128), f32),
         ),
-        in_specs=[spec(pltpu.SMEM)] * 2 + [spec()] * 8 + [spec(pltpu.HBM)] * 7,
+        in_specs=[spec(pltpu.SMEM)] * 2 + [spec()] * 16,
         out_specs=(spec(),) * 3,
         scratch_shapes=[
             pltpu.VMEM((1024, 128), f32),
@@ -437,16 +472,11 @@
             pltpu.VMEM((512, 512), bf16),
             pltpu.VMEM((512, 128), f32),
             pltpu.VMEM((4096, 1024), bf16),
-            pltpu.VMEM((4096, 128), f32),
+            pltpu.VMEM((2048, 128), f32),
             pltpu.VMEM((128, 4096), bf16),
-            pltpu.VMEM((1024, 128), bf16),
-            pltpu.VMEM((128, 1024), bf16),
-            pltpu.VMEM((128, 1024), bf16),
-            pltpu.VMEM((1024, 128), f32),
-        ]
-        + held(*others),
+        ],
         compiler_params=limit(24),
-    )(place, scale, *pieces, *far(*others))
+    )(place, scale, *pieces, *others)
 
 
 def join_kernel(*refs):
@@ -478,13 +508,15 @@
     alignment, norm_gain, norm_bias, proj_weight, pair_weight, pair_bias, head_weight, head_bias,
     labels, pair_mask, loss_scale,
 ):
-    gain = norm_gain.reshape(1, 256)
-    message = prepare(alignment, gain, norm_bias.reshape(1, 256), proj_weight.T, labels.T, pair_mask.T)
+    message, align, gain, proj_t, pair, pair_bias, head_t, head_bias = prepare(
+        alignment, norm_gain.reshape(1, 256), proj_weight.T, norm_bias.reshape(1, 256), labels.T, pair_mask.T,
+        pair_weight, pair_bias.reshape(1, 128), head_weight.T, head_bias.reshape(1, 64),
+    )
+    arranged = weights(pair, pair_bias, head_t, head_bias)
     pieces = gather(message)
     place = lax.axis_index(("row", "col")).astype(jnp.int32).reshape(1)
     loss, align_grad, weight_grad = pairs(
-        place, loss_scale.reshape(1), pieces, pair_weight, pair_bias.reshape(1, 128), head_weight.T,
-        head_bias.reshape(1, 64), alignment, gain, proj_weight.T,
+        place, loss_scale.reshape(1), pieces, *arranged, head_t, align, gain, proj_t
     )
     return (loss.reshape(()), align_grad, weight_grad)
 

time: 31.5 us -> 29.8 us (0.946)
  Pallas kernels: 12.3 us -> 11.2 us
  waiting for transfers between devices: 8.33 us -> 7.76 us
    pallas_call x1, Pallas kernels: 11 us -> 9.27 us  [pairs(): pl.pallas_call(pairs_kernel, out_shape=(jax.ShapeDtypeStruct((1, 1), f32)...]
    pallas_call x1 -> x2, Pallas kernels: 1.28 us -> 1.9 us  [the longest x1 1.31 us: prepare(): pl.pallas_call(prepare_kernel, out_shape=[jax.ShapeDtypeStruct((64, 128),...]
    ppermute x10, waiting for transfers between devices: 8.33 us -> 7.76 us  [swap(): return lax.ppermute(block, ('row', 'col'), moves)]
  transfers between devices with their start and end apart: 10 -> 10, of which waited for: 6 -> 5; matrix products, arithmetic and copies ran while one was open for 0% -> 0% of each run, Pallas kernels for 0% -> 2%
where the time goes in v3:
time: 29.8 us; the launch traced here: 29.6 us
  Pallas kernels  11.2 us (38%)
  starting transfers between devices  9.32 us (31%)
  waiting for transfers between devices  7.76 us (26%)
  between operations  1.35 us (5%)
    ppermute x10, starting transfers between devices, swap(): return lax.ppermute(block, ('row', 'col'), moves)  9.32 us
    pallas_call x1, Pallas kernels, pairs(): pl.pallas_call(pairs_kernel, out_shape=(jax.ShapeDtypeStruct((1, 1), f32)...  9.27 us
    ppermute x10, waiting for transfers between devices, swap(): return lax.ppermute(block, ('row', 'col'), moves)  7.76 us
    pallas_call x1, Pallas kernels, prepare(): pl.pallas_call(prepare_kernel, out_shape=[jax.ShapeDtypeStruct((64, 128),...  1.31 us
  transfers between devices with their start and end apart: 10, of which 5 were waited for; matrix products, arithmetic and copies ran while one was open for 0% of the time, Pallas kernels for 2%

profile of v3, /device:TPU:0, one launch (start us, length us, event | category | flops | bytes accessed | tf_op | source)
XLA Modules:
  0.0 29.6 jit_solution(3785891435692488146)
XLA Ops:
  0.6 1.3 %shard_map.130 = (bf16[64,128]{1,0:T(8,128)(2,1)S(1)}, bf16[32,2,256]{2,1,0:T(2,128)(2,1)S(1)}, f32[1,256]{1,0:T(1,128)S(1)}, bf16[64,256]{1,0:T(8,128)(2,1)S(1)...) custom-call(bf16[32,2,256]{2,1,0:T(2,128)(2,1)} %refs_0_.1, ...), custom_call_target="tpu_custom_call" | custom-call | tf_op jit(solution)/shard_map/pallas_call | solution.py:432
  2.0 5.1 %collective-permute-start.2 = (bf16[64,128]{1,0:T(8,128)(2,1)S(1)}, bf16[64,128]{1,0:T(8,128)(2,1)S(1)}, u32[]{:S(2)}, u32[]{:S(2)}) collective-permute-start(bf16[64,128]{1,0:T(8,128)(2,1)S(1)} %get-tuple-element.18.refs_0_), channel_id=1, source_target_pairs={{0,6},{1,7},{2,4},{3,5},{4,2},{5,3},{6,0},{7,1},{8,14},{9,15},{10,... | collective-permute-start | bytes 49160 | tf_op jit(solution)/shard_map/ppermute | solution.py:500
  7.1 0.0 collective-permute-start.1
  7.1 0.6 %collective-permute-start = (bf16[64,128]{1,0:T(8,128)(2,1)S(1)}, bf16[64,128]{1,0:T(8,128)(2,1)S(1)}, u32[]{:S(2)}, u32[]{:S(2)}) collective-permute-start(bf16[64,128]{1,0:T(8,128)(2,1)S(1)} %get-tuple-element.18.refs_0_), channel_id=1, source_target_pairs={{0,2},{1,3},{2,0},{3,1},{4,6},{5,7},{6,4},{7,5},{8,10},{9,11},{10,... | collective-permute-start | bytes 49160 | tf_op jit(solution)/shard_map/ppermute | solution.py:500
  7.7 1.1 %collective-permute-done.2.refs_3_ = bf16[64,128]{1,0:T(8,128)(2,1)S(1)} collective-permute-done((bf16[64,128]{1,0:T(8,128)(2,1)S(1)}, bf16[64,128]{1,0:T(8,128)(2,1)S(1)}, u32[]{:S(2)}, u32[]{:S(2)}) %collective-permute-start.2) | collective-permute-done | bytes 16416 | tf_op jit(solution)/shard_map/ppermute | solution.py:500
  8.8 2.9 %collective-permute-done.1.refs_2_ = bf16[64,128]{1,0:T(8,128)(2,1)S(1)} collective-permute-done((bf16[64,128]{1,0:T(8,128)(2,1)S(1)}, bf16[64,128]{1,0:T(8,128)(2,1)S(1)}, u32[]{:S(2)}, u32[]{:S(2)}) %collective-permute-start.1) | collective-permute-done | bytes 16416 | tf_op jit(solution)/shard_map/ppermute | solution.py:500
  11.7 0.0 collective-permute-done.refs_1_
  11.7 2.5 %collective-permute-start.5 = (bf16[256,128]{1,0:T(8,128)(2,1)S(1)}, bf16[256,128]{1,0:T(8,128)(2,1)S(1)}, u32[]{:S(2)}, u32[]{:S(2)}) collective-permute-start(bf16[256,128]{1,0:T(8,128)(2,1)S(1)} %shard_map.131.refs_0_), channel_id=1, source_target_pairs={{0,17},{1,16},{2,19},{3,18},{4,21},{5,20},{6,23},{7,22},{8,25},{9,... | collective-permute-start | bytes 196616 | tf_op jit(solution)/shard_map/ppermute | solution.py:500
  14.2 0.5 %collective-permute-start.4 = (bf16[256,128]{1,0:T(8,128)(2,1)S(1)}, bf16[256,128]{1,0:T(8,128)(2,1)S(1)}, u32[]{:S(2)}, u32[]{:S(2)}) collective-permute-start(bf16[256,128]{1,0:T(8,128)(2,1)S(1)} %shard_map.131.refs_0_), channel_id=1, source_target_pairs={{0,16},{1,17},{2,18},{3,19},{4,20},{5,21},{6,22},{7,23},{8,24},{9,... | collective-permute-start | bytes 196616 | tf_op jit(solution)/shard_map/ppermute | solution.py:500
  14.8 0.5 %collective-permute-start.3 = (bf16[256,128]{1,0:T(8,128)(2,1)S(1)}, bf16[256,128]{1,0:T(8,128)(2,1)S(1)}, u32[]{:S(2)}, u32[]{:S(2)}) collective-permute-start(bf16[256,128]{1,0:T(8,128)(2,1)S(1)} %shard_map.131.refs_0_), channel_id=1, source_target_pairs={{0,1},{1,0},{2,3},{3,2},{4,5},{5,4},{6,7},{7,6},{8,9},{9,8},{10,11... | collective-permute-start | bytes 196616 | tf_op jit(solution)/shard_map/ppermute | solution.py:500
  15.3 0.0 collective-permute-start.6
  15.3 1.7 %collective-permute-done.5.refs_3_ = bf16[256,128]{1,0:T(8,128)(2,1)S(1)} collective-permute-done((bf16[256,128]{1,0:T(8,128)(2,1)S(1)}, bf16[256,128]{1,0:T(8,128)(2,1)S(1)}, u32[]{:S(2)}, u32[]{:S(2)}) %collective-permute-start.5) | collective-permute-done | bytes 65568 | tf_op jit(solution)/shard_map/ppermute | solution.py:500
  16.9 0.0 collective-permute-start.9
  17.0 1.5 %collective-permute-done.4.refs_2_ = bf16[256,128]{1,0:T(8,128)(2,1)S(1)} collective-permute-done((bf16[256,128]{1,0:T(8,128)(2,1)S(1)}, bf16[256,128]{1,0:T(8,128)(2,1)S(1)}, u32[]{:S(2)}, u32[]{:S(2)}) %collective-permute-start.4) | collective-permute-done | bytes 65568 | tf_op jit(solution)/shard_map/ppermute | solution.py:500
  18.5 0.0 collective-permute-start.8
  18.5 0.5 %collective-permute-done.3.refs_1_ = bf16[256,128]{1,0:T(8,128)(2,1)S(1)} collective-permute-done((bf16[256,128]{1,0:T(8,128)(2,1)S(1)}, bf16[256,128]{1,0:T(8,128)(2,1)S(1)}, u32[]{:S(2)}, u32[]{:S(2)}) %collective-permute-start.3) | collective-permute-done | bytes 65568 | tf_op jit(solution)/shard_map/ppermute | solution.py:500
  19.0 0.0 collective-permute-start.7
  19.7 0.6 %shard_map.132 = (bf16[1024,128]{1,0:T(8,128)(2,1)S(1)}, bf16[128,1024]{1,0:T(8,128)(2,1)S(1)}, bf16[128,1024]{1,0:T(8,128)(2,1)S(1)}, f32[64,1]{1,0:T(8,128)S(1)}) custom-call(bf16[1024,128]{1,0:T(8,128)(2,1)S(1)} %get-tuple-element.19.pair_ref, f32[1,128]{1,0:T(1,128)S(1)} %get-tuple-element.20.pair_bias_ref, ...), custom_call_target="tpu_custom_call" | custom-call | tf_op jit(solution)/shard_map/pallas_call | solution.py:443
  20.3 0.0 collective-permute-done.6.refs_4_
  20.3 0.0 collective-permute-done.9.refs_7_
  20.3 0.0 collective-permute-done.8.refs_6_
  20.3 0.0 collective-permute-done.7.refs_5_
  20.3 9.3 %shard_map.133 = (f32[1,1]{1,0:T(1,128)}, f32[32,2,256]{2,1,0:T(2,128)}, f32[1024,128]{1,0:T(8,128)}) custom-call(s32[1]{0:T(128)} %bitcast.place_ref, f32[1]{0:T(128)} %bitcast.11.scale_ref, bf16[256,128]{1,0:T(8,128)(2,1)S(1)} %shard_map.131.refs_0_, bf16[256,128]{1,0:T(8,128)(2,1)S(1)} %collective-permute-done.3.refs_1_, ...), custom_call_target="tpu_custom_call" | custom-call | tf_op jit(solution)/shard_map/pallas_call | solution.py:459
  (1 shorter events, 0.0 us)
Async XLA Ops:
  2.0 6.8 %collective-permute-start.2 = (bf16[64,128]{1,0:T(8,128)(2,1)S(1)}, bf16[64,128]{1,0:T(8,128)(2,1)S(1)}, u32[]{:S(2)}, u32[]{:S(2)}) collective-permute-start(bf16[64,128]{1,0:T(8,128)(2,1)S(1)} %get-tuple-element.18.refs_0_), channel_id=1, source_target_pairs={{0,6},{1,7},{2,4},{3,5},{4,2},{5,3},{6,0},{7,1},{8,14},{9,15},{10,... | collective-permute-start | bytes 49160 | tf_op jit(solution)/shard_map/ppermute | solution.py:500
  7.1 4.6 %collective-permute-start.1 = (bf16[64,128]{1,0:T(8,128)(2,1)S(1)}, bf16[64,128]{1,0:T(8,128)(2,1)S(1)}, u32[]{:S(2)}, u32[]{:S(2)}) collective-permute-start(bf16[64,128]{1,0:T(8,128)(2,1)S(1)} %get-tuple-element.18.refs_0_), channel_id=1, source_target_pairs={{0,4},{1,5},{2,6},{3,7},{4,0},{5,1},{6,2},{7,3},{8,12},{9,13},{10,... | collective-permute-start | bytes 49160 | tf_op jit(solution)/shard_map/ppermute | solution.py:500
  7.1 4.6 %collective-permute-start = (bf16[64,128]{1,0:T(8,128)(2,1)S(1)}, bf16[64,128]{1,0:T(8,128)(2,1)S(1)}, u32[]{:S(2)}, u32[]{:S(2)}) collective-permute-start(bf16[64,128]{1,0:T(8,128)(2,1)S(1)} %get-tuple-element.18.refs_0_), channel_id=1, source_target_pairs={{0,2},{1,3},{2,0},{3,1},{4,6},{5,7},{6,4},{7,5},{8,10},{9,11},{10,... | collective-permute-start | bytes 49160 | tf_op jit(solution)/shard_map/ppermute | solution.py:500
  11.7 5.2 %collective-permute-start.5 = (bf16[256,128]{1,0:T(8,128)(2,1)S(1)}, bf16[256,128]{1,0:T(8,128)(2,1)S(1)}, u32[]{:S(2)}, u32[]{:S(2)}) collective-permute-start(bf16[256,128]{1,0:T(8,128)(2,1)S(1)} %shard_map.131.refs_0_), channel_id=1, source_target_pairs={{0,17},{1,16},{2,19},{3,18},{4,21},{5,20},{6,23},{7,22},{8,25},{9,... | collective-permute-start | bytes 196616 | tf_op jit(solution)/shard_map/ppermute | solution.py:500
  14.2 4.3 %collective-permute-start.4 = (bf16[256,128]{1,0:T(8,128)(2,1)S(1)}, bf16[256,128]{1,0:T(8,128)(2,1)S(1)}, u32[]{:S(2)}, u32[]{:S(2)}) collective-permute-start(bf16[256,128]{1,0:T(8,128)(2,1)S(1)} %shard_map.131.refs_0_), channel_id=1, source_target_pairs={{0,16},{1,17},{2,18},{3,19},{4,20},{5,21},{6,22},{7,23},{8,24},{9,... | collective-permute-start | bytes 196616 | tf_op jit(solution)/shard_map/ppermute | solution.py:500
  14.8 4.3 %collective-permute-start.3 = (bf16[256,128]{1,0:T(8,128)(2,1)S(1)}, bf16[256,128]{1,0:T(8,128)(2,1)S(1)}, u32[]{:S(2)}, u32[]{:S(2)}) collective-permute-start(bf16[256,128]{1,0:T(8,128)(2,1)S(1)} %shard_map.131.refs_0_), channel_id=1, source_target_pairs={{0,1},{1,0},{2,3},{3,2},{4,5},{5,4},{6,7},{7,6},{8,9},{9,8},{10,11... | collective-permute-start | bytes 196616 | tf_op jit(solution)/shard_map/ppermute | solution.py:500
  15.3 5.0 %collective-permute-start.6 = (bf16[256,128]{1,0:T(8,128)(2,1)S(1)}, bf16[256,128]{1,0:T(8,128)(2,1)S(1)}, u32[]{:S(2)}, u32[]{:S(2)}) collective-permute-start(bf16[256,128]{1,0:T(8,128)(2,1)S(1)} %shard_map.131.refs_0_), channel_id=1, source_target_pairs={{0,8},{1,9},{2,10},{3,11},{4,12},{5,13},{6,14},{7,15},{8,0},{9,1},... | collective-permute-start | bytes 196616 | tf_op jit(solution)/shard_map/ppermute | solution.py:500
  16.9 3.3 %collective-permute-start.9 = (bf16[256,128]{1,0:T(8,128)(2,1)S(1)}, bf16[256,128]{1,0:T(8,128)(2,1)S(1)}, u32[]{:S(2)}, u32[]{:S(2)}) collective-permute-start(bf16[256,128]{1,0:T(8,128)(2,1)S(1)} %collective-permute-done.5.refs_3_), channel_id=1, source_target_pairs={{0,8},{1,9},{2,10},{3,11},{4,12},{5,13},{6,14},{7,15},{8,0},{9,1},... | collective-permute-start | bytes 196616 | tf_op jit(solution)/shard_map/ppermute | solution.py:500
  18.5 1.8 %collective-permute-start.8 = (bf16[256,128]{1,0:T(8,128)(2,1)S(1)}, bf16[256,128]{1,0:T(8,128)(2,1)S(1)}, u32[]{:S(2)}, u32[]{:S(2)}) collective-permute-start(bf16[256,128]{1,0:T(8,128)(2,1)S(1)} %collective-permute-done.4.refs_2_), channel_id=1, source_target_pairs={{0,8},{1,9},{2,10},{3,11},{4,12},{5,13},{6,14},{7,15},{8,0},{9,1},... | collective-permute-start | bytes 196616 | tf_op jit(solution)/shard_map/ppermute | solution.py:500
  19.0 1.3 %collective-permute-start.7 = (bf16[256,128]{1,0:T(8,128)(2,1)S(1)}, bf16[256,128]{1,0:T(8,128)(2,1)S(1)}, u32[]{:S(2)}, u32[]{:S(2)}) collective-permute-start(bf16[256,128]{1,0:T(8,128)(2,1)S(1)} %collective-permute-done.3.refs_1_), channel_id=1, source_target_pairs={{0,8},{1,9},{2,10},{3,11},{4,12},{5,13},{6,14},{7,15},{8,0},{9,1},... | collective-permute-start | bytes 196616 | tf_op jit(solution)/shard_map/ppermute | solution.py:500

commit v4 on v3

--- a/solution.py
+++ b/solution.py
@@ -252,29 +252,30 @@
     bias_ref[...] = 2.0 * (jnp.sum(head_t.astype(f32) * pair_bias_ref[...], axis=1, keepdims=True) + own_bias)
 
 
-def pairs_kernel(
-    place_ref, scale_ref, *refs
-):
+def pairs_kernel(place_ref, scale_ref, *refs):
     pieces, refs = refs[:8], refs[8:]
     (
-        folded_ref, by_left_ref, by_right_ref, bias_ref, head_ref, align_ref, gain_ref, proj_ref,
-        loss_ref, align_grad_ref, weight_grad_ref,
+        folded_ref, bias_ref, head_ref, grad_ref, note_ref, groups_ref,
         turned_ref, left_ref, plain_ref, wide_ref, flat_ref, features_ref, half_ref, dhidden_ref,
     ) = refs
     place = place_ref[0]
+    core = place // core_move % 2
     for n, piece in enumerate(pieces):
         for k in range(4):
-            sender = place ^ (n // 4 * 8 + n // 2 % 2 * 16 + n % 2 + k * 2)
+            sender = place ^ (first_moves[k] ^ second_moves[n % 4] ^ n // 4 * core_move)
             at = k * 64
             turned_ref[pl.ds(pl.multiple_of(sender * 32, 32), 32), :] = piece[at : at + 32, :].astype(f32)
             plain_ref[pl.ds(pl.multiple_of(sender * 16, 16), 16), :] = piece[at + 32 : at + 48, :]
             flat_ref[pl.ds(pl.multiple_of(sender * 16, 16), 16), :] = piece[at + 48 : at + 64, :].astype(f32)
-    groups = [
-        jnp.concatenate([turned_ref[pl.ds(p * 16 + g, 32, stride=32), :] for p in range(2)], axis=0).astype(bf16)
-        for g in range(16)
-    ]
-    for g in range(8):
-        left_ref[g * 64 : g * 64 + 64, :] = groups[g]
+    for g in range(16):
+        for p in range(2):
+            groups_ref[p * 32 : p * 32 + 32, g * 128 : g * 128 + 128] = turned_ref[
+                pl.ds(p * 16 + g, 32, stride=32), :
+            ].astype(bf16)
+    for q in range(2):
+        for g in range(8):
+            at = (q * 8 + g) * 32
+            left_ref[at : at + 32, :] = turned_ref[pl.ds((core + q) % 2 * 16 + g, 32, stride=32), :].astype(bf16)
     source = lax.broadcasted_iota(jnp.int32, (128, 512), 0)
     target = lax.broadcasted_iota(jnp.int32, (128, 512), 1)
     copies = jnp.where(source == target // 128 * 32 + target % 32, 1.0 / 32.0, 0.0).astype(bf16)
@@ -282,97 +283,99 @@
 
     lane = lax.broadcasted_iota(jnp.int32, (32, 128), 1) // 32
 
-    def outer_products(d):
+    def outer_products(k, q):
         sides = []
-        for r in range(2):
+        for d in (2 * k, 2 * k + 1):
             right = jnp.concatenate(
-                [wide_ref[d * 16 : d * 16 + 16, (h * 2 + r) * 128 : (h * 2 + r + 1) * 128] for h in range(2)], axis=0
+                [wide_ref[d * 16 : d * 16 + 16, (h * 2 + q) * 128 : (h * 2 + q + 1) * 128] for h in range(2)], axis=0
             )
             sides.append(
-                jnp.concatenate([jnp.where(lane == q, right, jnp.zeros_like(right)) for q in range(4)], axis=0)
+                jnp.concatenate([jnp.where(lane == c, right, jnp.zeros_like(right)) for c in range(4)], axis=0)
             )
-        outer = dot(left_ref[...], jnp.concatenate(sides, axis=1)).astype(bf16)
-        for r in range(2):
-            for p in range(2):
-                at = d // 2 * 256 + (p + r) % 2 * 128 + d % 2 * 64 + r * 32
-                for g in range(8):
-                    features_ref[at : at + 32, g * 128 : g * 128 + 128] = outer[
-                        g * 64 + p * 32 : g * 64 + p * 32 + 32, r * 128 : r * 128 + 128
-                    ]
-
-    side = lax.broadcasted_iota(jnp.int32, (128, 128), 1) < 64
-
-    def half_logits(d):
-        at = d // 2 * 256 + d % 2 * 64
-        rows = jnp.concatenate([features_ref[at + h : at + h + 64, :] for h in (0, 128)], axis=0)
-        part = dot(rows, folded_ref[...])
-        part = part + pltpu.roll(part, 64, 1)
-        half_ref[d * 64 : d * 64 + 64, :] = jnp.where(side[0:64], part[0:64], part[64:128])
-
-    early = 2
-    for d in range(early):
-        outer_products(d)
-    for d in range(32):
-        if d + early < 32:
-            outer_products(d + early)
-        half_logits(d)
-
-    source = lax.broadcasted_iota(jnp.int32, (128, 1024), 0)
-    target = lax.broadcasted_iota(jnp.int32, (128, 1024), 1)
-    first = target // 256 * 4 + target // 32 % 4
-    second = target % 32 * 2 + (target // 128 + first) % 2
+        outer = dot(left_ref[q * 256 : q * 256 + 256, :], jnp.concatenate(sides, axis=1)).astype(bf16)
+        for e in range(2):
+            at = k * 128 + e * 64 + q * 32
+            for g in range(8):
+                features_ref[at : at + 32, g * 128 : g * 128 + 128] = outer[
+                    g * 32 : g * 32 + 32, e * 128 : e * 128 + 128
+                ]
+
+    early = 1
+    for k in range(16 + early):
+        if k < 16:
+            outer_products(k, 0)
+            outer_products(k, 1)
+        if k >= early:
+            at = (k - early) * 128
+            half_ref[at : at + 128, :] = dot(features_ref[at : at + 128, :], folded_ref[...])
+
+    source = lax.broadcasted_iota(jnp.int32, (128, 512), 0)
+    target = lax.broadcasted_iota(jnp.int32, (128, 512), 1)
+    first = target // 128 * 4 + target // 32 % 4
+    second = target % 32 * 2 + (core + first) % 2
     spread = (source == first * 8 + second % 8).astype(bf16)
-    keep = second[0:32] // 8 == lax.broadcasted_iota(jnp.int32, (32, 1024), 0) % 8
+    keep = second[0:32] // 8 == lax.broadcasted_iota(jnp.int32, (32, 512), 0) % 8
 
     def blocks(row):
         placed = dot(flat_ref[pl.ds(row, 32, stride=16), :].astype(bf16), spread)
-        return jnp.sum(jnp.where(keep, placed, 0.0).reshape(4, 8, 1024), axis=1)
+        return jnp.sum(jnp.where(keep, placed, 0.0).reshape(4, 8, 512), axis=1)
 
     labels = blocks(0).astype(jnp.int32)
     mask = blocks(1)
-    valid = jnp.sum(mask, keepdims=True)
+    valid = jnp.sum(flat_ref[pl.ds(1, 32, stride=16), :], keepdims=True)
     factor = mask * (scale_ref[0] / valid)
     head2 = (2.0 * head_ref[...].astype(f32).T).astype(bf16)
     bins = lax.broadcasted_iota(jnp.int32, (64, 256), 0)
     loss = jnp.zeros((1, 256), f32)
-    for k in range(16):
-        rows = []
-        for j in (k * 2, k * 2 + 1):
-            even = half_ref[pl.ds(j, 32, stride=64), :]
-            odd = half_ref[pl.ds(j + 32, 32, stride=64), :]
-            rows += [jnp.where(side[0:32], even, odd), jnp.where(side[0:32], odd, even)]
-        both = (half_ref[k * 128 : k * 128 + 128, :] + jnp.concatenate(rows, axis=0)).T
-        logits = jnp.concatenate([both[0:64], both[64:128]], axis=1) + bias_ref[...]
-        part = slice(k % 4 * 256, k % 4 * 256 + 256)
-        labels_here = labels[k // 4 : k // 4 + 1, part]
+    for k in range(8):
+        tiles = []
+        for d in (4 * k, 4 * k + 2):
+            rows = [
+                half_ref[pl.ds((core + q) % 2 * 32 + d + e, 32, stride=64), :] for e in range(2) for q in range(2)
+            ]
+            both = (half_ref[d * 64 : d * 64 + 128, :] + jnp.concatenate(rows, axis=0)).T
+            tiles.append(both[0:64] + both[64:128])
+        logits = jnp.concatenate(tiles, axis=1) + bias_ref[...]
+        part = (slice(k // 2, k // 2 + 1), slice(k % 2 * 256, k % 2 * 256 + 256))
         shifted = logits - jnp.max(logits, axis=0, keepdims=True)
         exp_shift = jnp.exp(shifted)
         exp_total = jnp.sum(exp_shift, axis=0, keepdims=True)
-        hit = bins == labels_here
+        hit = bins == labels[part]
         picked = jnp.sum(jnp.where(hit, shifted, 0.0), axis=0, keepdims=True)
-        loss = loss + mask[k // 4 : k // 4 + 1, part] * (jnp.log(exp_total) - picked)
-        here = factor[k // 4 : k // 4 + 1, part]
+        loss = loss + mask[part] * (jnp.log(exp_total) - picked)
+        here = factor[part]
         dlogits = exp_shift * (here / exp_total) - jnp.where(hit, here, 0.0)
         dhidden_ref[:, k * 256 : k * 256 + 256] = dot(head2, dlogits.astype(bf16)).astype(bf16)
-    loss_ref[...] = jnp.sum(loss, axis=1, keepdims=True) / valid
+
+    def of_device(d):
+        columns = dhidden_ref[:, pl.ds(pl.multiple_of(d // 2 * 128, 128), 128)].astype(f32)
+        return jnp.where(d % 2 == 0, columns[:, 0:64], columns[:, 64:128])
+
+    note_ref[0:128, :] = jnp.concatenate([of_device(place ^ core_move), of_device(place)], axis=1)
+    note_ref[128:136, :] = jnp.broadcast_to(jnp.sum(loss, axis=1, keepdims=True) / valid, (8, 128))
 
     for n in range(4):
-        turned = dot(dhidden_ref[...], features_ref[:, n * 256 : n * 256 + 256]).T
+        turned = dot(dhidden_ref[...], features_ref[:, n * 256 : n * 256 + 256]).T.astype(bf16)
         for g in range(2):
             for q in range(4):
                 at = (q * 8 + n * 2 + g) * 32
-                weight_grad_ref[at : at + 32, :] = turned[g * 128 + q * 32 : g * 128 + q * 32 + 32]
-
-    own = dhidden_ref[:, pl.ds(pl.multiple_of(place // 2 * 256, 256), 256)]
-    own = [jnp.where(place % 2 == 0, own[:, n : n + 64], own[:, n + 64 : n + 128]) for n in (0, 128)]
-    own = jnp.concatenate(
-        [
-            jnp.concatenate([own[0][:, 0:32], own[1][:, 0:32]], axis=1),
-            jnp.concatenate([own[1][:, 32:64], own[0][:, 32:64]], axis=1),
-        ],
-        axis=0,
-    )
-    sums = dot(own, jnp.concatenate(groups, axis=1)).astype(bf16)
+                grad_ref[at : at + 32, :] = turned[g * 128 + q * 32 : g * 128 + q * 32 + 32]
+
+
+def finish_kernel(
+    place_ref, part_ref, other_part_ref, note_ref, other_ref, groups_ref, by_left_ref, by_right_ref,
+    align_ref, gain_ref, proj_ref, loss_ref, align_grad_ref, weight_grad_ref,
+):
+    weight_grad_ref[...] = part_ref[...].astype(f32) + other_part_ref[...].astype(f32)
+    core = place_ref[0] // core_move % 2
+    loss_ref[...] = note_ref[128:129, 0:1] + other_ref[128:129, 0:1]
+    mine, other = note_ref[0:128, 64:128], other_ref[0:128, 0:64]
+    own = []
+    for q in range(2):
+        a, b = mine[:, q * 32 : q * 32 + 32], other[:, q * 32 : q * 32 + 32]
+        odd = (core + q) % 2 == 1
+        own.append(jnp.concatenate([jnp.where(odd, b, a), jnp.where(odd, a, b)], axis=1))
+    sums = dot(jnp.concatenate(own, axis=0).astype(bf16), groups_ref[...]).astype(bf16)
 
     def contract(weights, base):
         q_rows = jnp.concatenate(
@@ -459,11 +462,11 @@
     return pl.pallas_call(
         pairs_kernel,
         out_shape=(
-            jax.ShapeDtypeStruct((1, 1), f32),
-            jax.ShapeDtypeStruct((32, 2, 256), f32),
-            jax.ShapeDtypeStruct((1024, 128), f32),
+            jax.ShapeDtypeStruct((1024, 128), bf16),
+            jax.ShapeDtypeStruct((136, 128), f32),
+            jax.ShapeDtypeStruct((64, 2048), bf16),
         ),
-        in_specs=[spec(pltpu.SMEM)] * 2 + [spec()] * 16,
+        in_specs=[spec(pltpu.SMEM)] * 2 + [spec()] * 11,
         out_specs=(spec(),) * 3,
         scratch_shapes=[
             pltpu.VMEM((1024, 128), f32),
@@ -471,12 +474,26 @@
             pltpu.VMEM((512, 128), bf16),
             pltpu.VMEM((512, 512), bf16),
             pltpu.VMEM((512, 128), f32),
-            pltpu.VMEM((4096, 1024), bf16),
+            pltpu.VMEM((2048, 1024), bf16),
             pltpu.VMEM((2048, 128), f32),
-            pltpu.VMEM((128, 4096), bf16),
+            pltpu.VMEM((128, 2048), bf16),
         ],
-        compiler_params=limit(24),
+        compiler_params=limit(20),
     )(place, scale, *pieces, *others)
+
+
+def finish(place, *others):
+    return pl.pallas_call(
+        finish_kernel,
+        out_shape=(
+            jax.ShapeDtypeStruct((1, 1), f32),
+            jax.ShapeDtypeStruct((32, 2, 256), f32),
+            jax.ShapeDtypeStruct((1024, 128), f32),
+        ),
+        in_specs=[spec(pltpu.SMEM)] + [spec()] * 10,
+        out_specs=(spec(),) * 3,
+        compiler_params=limit(8),
+    )(place, *others)
 
 
 def join_kernel(*refs):
@@ -494,14 +511,19 @@
     )(*parts)
 
 
+first_moves = (0, 2, 4, 6)
+second_moves = (0, 1, 16, 17)
+core_move = 8
+
+
+def swap(block, move):
+    return lax.ppermute(block, ("row", "col"), [(d, d ^ move) for d in range(32)])
+
+
 def gather(message):
-    def swap(block, row_bits, col_bits):
-        moves = [(d, (d // 8 ^ row_bits) * 8 + (d % 8 ^ col_bits)) for d in range(32)]
-        return lax.ppermute(block, ("row", "col"), moves)
-
-    line = join([message] + [swap(message, 0, 2 * k) for k in range(1, 4)])
-    plane = [line] + [swap(line, n // 2 * 2, n % 2) for n in range(1, 4)]
-    return plane + [swap(block, 1, 0) for block in plane]
+    line = join([message] + [swap(message, move) for move in first_moves[1:]])
+    plane = [line] + [swap(line, move) for move in second_moves[1:]]
+    return plane + [swap(block, core_move) for block in plane]
 
 
 def local_whole(
@@ -512,11 +534,13 @@
         alignment, norm_gain.reshape(1, 256), proj_weight.T, norm_bias.reshape(1, 256), labels.T, pair_mask.T,
         pair_weight, pair_bias.reshape(1, 128), head_weight.T, head_bias.reshape(1, 64),
     )
-    arranged = weights(pair, pair_bias, head_t, head_bias)
+    folded, by_left, by_right, bias = weights(pair, pair_bias, head_t, head_bias)
     pieces = gather(message)
     place = lax.axis_index(("row", "col")).astype(jnp.int32).reshape(1)
-    loss, align_grad, weight_grad = pairs(
-        place, loss_scale.reshape(1), pieces, *arranged, head_t, align, gain, proj_t
+    part, note, groups = pairs(place, loss_scale.reshape(1), pieces, folded, bias, head_t)
+    loss, align_grad, weight_grad = finish(
+        place, part, swap(part, core_move), note, swap(note, core_move), groups, by_left, by_right,
+        align, gain, proj_t,
     )
     return (loss.reshape(()), align_grad, weight_grad)
 

time: 29.8 us -> 29.3 us (0.983)
  Pallas kernels: 11.2 us -> 8.86 us
  waiting for transfers between devices: 7.76 us -> 8.94 us
  starting transfers between devices: 9.32 us -> 9.97 us
    pallas_call x1 -> x2, Pallas kernels: 9.27 us -> 6.96 us  [the longest x1 4.96 us: pairs(): pl.pallas_call(pairs_kernel, out_shape=(jax.ShapeDtypeStruct((1024, 128),...]
    ppermute x10 -> x12, waiting for transfers between devices: 7.76 us -> 8.94 us  [swap(): lax.ppermute(block, ('row', 'col'), [(d, d ^ move) for d in range(32)])]
    ppermute x10 -> x12, starting transfers between devices: 9.32 us -> 9.97 us  [swap(): lax.ppermute(block, ('row', 'col'), [(d, d ^ move) for d in range(32)])]
  transfers between devices with their start and end apart: 10 -> 12, of which waited for: 5 -> 6; matrix products, arithmetic and copies ran while one was open for 0% -> 0% of each run, Pallas kernels for 2% -> 2%
where the time goes in v4:
time: 29.3 us; the launch traced here: 29.1 us
  starting transfers between devices  9.97 us (34%)
  waiting for transfers between devices  8.94 us (31%)
  Pallas kernels  8.86 us (30%)
  between operations  1.36 us (5%)
    ppermute x12, starting transfers between devices, swap(): lax.ppermute(block, ('row', 'col'), [(d, d ^ move) for d in range(32)])  9.97 us
    ppermute x12, waiting for transfers between devices, swap(): lax.ppermute(block, ('row', 'col'), [(d, d ^ move) for d in range(32)])  8.94 us
    pallas_call x1, Pallas kernels, pairs(): pl.pallas_call(pairs_kernel, out_shape=(jax.ShapeDtypeStruct((1024, 128),...  4.96 us
    pallas_call x1, Pallas kernels, finish(): pl.pallas_call(finish_kernel, out_shape=(jax.ShapeDtypeStruct((1, 1), f32...  1.99 us
    pallas_call x1, Pallas kernels, prepare(): pl.pallas_call(prepare_kernel, out_shape=[jax.ShapeDtypeStruct((64, 128),...  1.31 us
    pallas_call x1, Pallas kernels, weights(): pl.pallas_call(weights_kernel, out_shape=(jax.ShapeDtypeStruct((1024, 128...  0.59 us
  transfers between devices with their start and end apart: 12, of which 6 were waited for; matrix products, arithmetic and copies ran while one was open for 0% of the time, Pallas kernels for 2%

profile of v4, /device:TPU:0, one launch (start us, length us, event | category | flops | bytes accessed | tf_op | source)
XLA Modules:
  0.0 29.1 jit_solution(8831864297641164904)
XLA Ops:
  0.6 1.3 %shard_map.130 = (bf16[64,128]{1,0:T(8,128)(2,1)S(1)}, bf16[32,2,256]{2,1,0:T(2,128)(2,1)S(1)}, f32[1,256]{1,0:T(1,128)S(1)}, bf16[64,256]{1,0:T(8,128)(2,1)S(1)...) custom-call(bf16[32,2,256]{2,1,0:T(2,128)(2,1)} %refs_0_.1, ...), custom_call_target="tpu_custom_call" | custom-call | tf_op jit(solution)/shard_map/pallas_call | solution.py:435
  2.0 5.1 %collective-permute-start.2 = (bf16[64,128]{1,0:T(8,128)(2,1)S(1)}, bf16[64,128]{1,0:T(8,128)(2,1)S(1)}, u32[]{:S(2)}, u32[]{:S(2)}) collective-permute-start(bf16[64,128]{1,0:T(8,128)(2,1)S(1)} %get-tuple-element.21.refs_0_), channel_id=1, source_target_pairs={{0,6},{1,7},{2,4},{3,5},{4,2},{5,3},{6,0},{7,1},{8,14},{9,15},{10,... | collective-permute-start | bytes 49160 | tf_op jit(solution)/shard_map/ppermute | solution.py:520
  7.1 0.0 collective-permute-start.1
  7.1 0.6 %collective-permute-start = (bf16[64,128]{1,0:T(8,128)(2,1)S(1)}, bf16[64,128]{1,0:T(8,128)(2,1)S(1)}, u32[]{:S(2)}, u32[]{:S(2)}) collective-permute-start(bf16[64,128]{1,0:T(8,128)(2,1)S(1)} %get-tuple-element.21.refs_0_), channel_id=1, source_target_pairs={{0,2},{1,3},{2,0},{3,1},{4,6},{5,7},{6,4},{7,5},{8,10},{9,11},{10,... | collective-permute-start | bytes 49160 | tf_op jit(solution)/shard_map/ppermute | solution.py:520
  7.7 1.1 %collective-permute-done.2.refs_3_ = bf16[64,128]{1,0:T(8,128)(2,1)S(1)} collective-permute-done((bf16[64,128]{1,0:T(8,128)(2,1)S(1)}, bf16[64,128]{1,0:T(8,128)(2,1)S(1)}, u32[]{:S(2)}, u32[]{:S(2)}) %collective-permute-start.2) | collective-permute-done | bytes 16416 | tf_op jit(solution)/shard_map/ppermute | solution.py:520
  8.8 2.9 %collective-permute-done.1.refs_2_ = bf16[64,128]{1,0:T(8,128)(2,1)S(1)} collective-permute-done((bf16[64,128]{1,0:T(8,128)(2,1)S(1)}, bf16[64,128]{1,0:T(8,128)(2,1)S(1)}, u32[]{:S(2)}, u32[]{:S(2)}) %collective-permute-start.1) | collective-permute-done | bytes 16416 | tf_op jit(solution)/shard_map/ppermute | solution.py:520
  11.7 0.0 collective-permute-done.refs_1_
  11.7 2.5 %collective-permute-start.5 = (bf16[256,128]{1,0:T(8,128)(2,1)S(1)}, bf16[256,128]{1,0:T(8,128)(2,1)S(1)}, u32[]{:S(2)}, u32[]{:S(2)}) collective-permute-start(bf16[256,128]{1,0:T(8,128)(2,1)S(1)} %shard_map.131.refs_0_), channel_id=1, source_target_pairs={{0,17},{1,16},{2,19},{3,18},{4,21},{5,20},{6,23},{7,22},{8,25},{9,... | collective-permute-start | bytes 196616 | tf_op jit(solution)/shard_map/ppermute | solution.py:520
  14.2 0.5 %collective-permute-start.4 = (bf16[256,128]{1,0:T(8,128)(2,1)S(1)}, bf16[256,128]{1,0:T(8,128)(2,1)S(1)}, u32[]{:S(2)}, u32[]{:S(2)}) collective-permute-start(bf16[256,128]{1,0:T(8,128)(2,1)S(1)} %shard_map.131.refs_0_), channel_id=1, source_target_pairs={{0,16},{1,17},{2,18},{3,19},{4,20},{5,21},{6,22},{7,23},{8,24},{9,... | collective-permute-start | bytes 196616 | tf_op jit(solution)/shard_map/ppermute | solution.py:520
  14.8 0.5 %collective-permute-start.3 = (bf16[256,128]{1,0:T(8,128)(2,1)S(1)}, bf16[256,128]{1,0:T(8,128)(2,1)S(1)}, u32[]{:S(2)}, u32[]{:S(2)}) collective-permute-start(bf16[256,128]{1,0:T(8,128)(2,1)S(1)} %shard_map.131.refs_0_), channel_id=1, source_target_pairs={{0,1},{1,0},{2,3},{3,2},{4,5},{5,4},{6,7},{7,6},{8,9},{9,8},{10,11... | collective-permute-start | bytes 196616 | tf_op jit(solution)/shard_map/ppermute | solution.py:520
  15.3 0.0 collective-permute-start.6
  15.3 1.7 %collective-permute-done.5.refs_3_ = bf16[256,128]{1,0:T(8,128)(2,1)S(1)} collective-permute-done((bf16[256,128]{1,0:T(8,128)(2,1)S(1)}, bf16[256,128]{1,0:T(8,128)(2,1)S(1)}, u32[]{:S(2)}, u32[]{:S(2)}) %collective-permute-start.5) | collective-permute-done | bytes 65568 | tf_op jit(solution)/shard_map/ppermute | solution.py:520
  16.9 0.0 collective-permute-start.9
  17.0 1.5 %collective-permute-done.4.refs_2_ = bf16[256,128]{1,0:T(8,128)(2,1)S(1)} collective-permute-done((bf16[256,128]{1,0:T(8,128)(2,1)S(1)}, bf16[256,128]{1,0:T(8,128)(2,1)S(1)}, u32[]{:S(2)}, u32[]{:S(2)}) %collective-permute-start.4) | collective-permute-done | bytes 65568 | tf_op jit(solution)/shard_map/ppermute | solution.py:520
  18.5 0.0 collective-permute-start.8
  18.5 0.5 %collective-permute-done.3.refs_1_ = bf16[256,128]{1,0:T(8,128)(2,1)S(1)} collective-permute-done((bf16[256,128]{1,0:T(8,128)(2,1)S(1)}, bf16[256,128]{1,0:T(8,128)(2,1)S(1)}, u32[]{:S(2)}, u32[]{:S(2)}) %collective-permute-start.3) | collective-permute-done | bytes 65568 | tf_op jit(solution)/shard_map/ppermute | solution.py:520
  19.0 0.0 collective-permute-start.7
  19.7 0.6 %shard_map.132 = (bf16[1024,128]{1,0:T(8,128)(2,1)S(1)}, bf16[128,1024]{1,0:T(8,128)(2,1)S(1)}, bf16[128,1024]{1,0:T(8,128)(2,1)S(1)}, f32[64,1]{1,0:T(8,128)S(1)}) custom-call(bf16[1024,128]{1,0:T(8,128)(2,1)S(1)} %get-tuple-element.22.pair_ref, f32[1,128]{1,0:T(1,128)S(1)} %get-tuple-element.23.pair_bias_ref, ...), custom_call_target="tpu_custom_call" | custom-call | tf_op jit(solution)/shard_map/pallas_call | solution.py:446
  20.3 0.0 collective-permute-done.6.refs_4_
  20.3 0.0 collective-permute-done.9.refs_7_
  20.3 0.0 collective-permute-done.8.refs_6_
  20.3 0.0 collective-permute-done.7.refs_5_
  20.3 5.0 %shard_map.133 = (bf16[1024,128]{1,0:T(8,128)(2,1)S(1)}, f32[136,128]{1,0:T(8,128)S(1)}, bf16[64,2048]{1,0:T(8,128)(2,1)S(1)}) custom-call(s32[1]{0:T(128)} %bitcast.place_ref, f32[1]{0:T(128)} %bitcast.11.scale_ref, bf16[256,128]{1,0:T(8,128)(2,1)S(1)} %shard_map.131.refs_0_, bf16[256,128]{1,0:T(8,128)(2,1)S(1)} %collective-permute-done.3.refs_1_, ...), custom_call_target="tpu_custom_call" | custom-call | tf_op jit(solution)/shard_map/pallas_call | solution.py:462
  25.3 0.6 %collective-permute-start.10 = (bf16[1024,128]{1,0:T(8,128)(2,1)S(1)}, bf16[1024,128]{1,0:T(8,128)(2,1)S(1)}, u32[]{:S(2)}, u32[]{:S(2)}) collective-permute-start(bf16[1024,128]{1,0:T(8,128)(2,1)S(1)} %get-tuple-element.28.part_ref), channel_id=1, source_target_pairs={{0,8},{1,9},{2,10},{3,11},{4,12},{5,13},{6,14},{7,15},{8,0},{9,1},... | collective-permute-start | bytes 786440 | tf_op jit(solution)/shard_map/ppermute | solution.py:520
  25.9 0.1 collective-permute-start.11
  25.9 1.2 %collective-permute-done.11.other_ref = f32[136,128]{1,0:T(8,128)S(1)} collective-permute-done((f32[136,128]{1,0:T(8,128)S(1)}, f32[136,128]{1,0:T(8,128)S(1)}, u32[]{:S(2)}, u32[]{:S(2)}) %collective-permute-start.11) | collective-permute-done | bytes 69664 | tf_op jit(solution)/shard_map/ppermute | solution.py:520
  27.1 0.0 collective-permute-done.10.other_part_ref
  27.1 2.0 %shard_map.134 = (f32[1,1]{1,0:T(1,128)}, f32[32,2,256]{2,1,0:T(2,128)}, f32[1024,128]{1,0:T(8,128)}) custom-call(s32[1]{0:T(128)} %bitcast.place_ref, bf16[1024,128]{1,0:T(8,128)(2,1)S(1)} %get-tuple-element.28.part_ref, bf16[1024,128]{1,0:T(8,128)(2,1)S(1)} %collective-permute-done.10.other_part_ref, f32[136,128]{1,0:T(8,128)S(1)} %get-tuple-element.29.note_ref, ...), custom_call_target="tpu_custom_call" | custom-call | tf_op jit(solution)/shard_map/pallas_call | solution.py:486
  (1 shorter events, 0.0 us)
Async XLA Ops:
  2.0 6.8 %collective-permute-start.2 = (bf16[64,128]{1,0:T(8,128)(2,1)S(1)}, bf16[64,128]{1,0:T(8,128)(2,1)S(1)}, u32[]{:S(2)}, u32[]{:S(2)}) collective-permute-start(bf16[64,128]{1,0:T(8,128)(2,1)S(1)} %get-tuple-element.21.refs_0_), channel_id=1, source_target_pairs={{0,6},{1,7},{2,4},{3,5},{4,2},{5,3},{6,0},{7,1},{8,14},{9,15},{10,... | collective-permute-start | bytes 49160 | tf_op jit(solution)/shard_map/ppermute | solution.py:520
  7.1 4.6 %collective-permute-start.1 = (bf16[64,128]{1,0:T(8,128)(2,1)S(1)}, bf16[64,128]{1,0:T(8,128)(2,1)S(1)}, u32[]{:S(2)}, u32[]{:S(2)}) collective-permute-start(bf16[64,128]{1,0:T(8,128)(2,1)S(1)} %get-tuple-element.21.refs_0_), channel_id=1, source_target_pairs={{0,4},{1,5},{2,6},{3,7},{4,0},{5,1},{6,2},{7,3},{8,12},{9,13},{10,... | collective-permute-start | bytes 49160 | tf_op jit(solution)/shard_map/ppermute | solution.py:520
  7.1 4.6 %collective-permute-start = (bf16[64,128]{1,0:T(8,128)(2,1)S(1)}, bf16[64,128]{1,0:T(8,128)(2,1)S(1)}, u32[]{:S(2)}, u32[]{:S(2)}) collective-permute-start(bf16[64,128]{1,0:T(8,128)(2,1)S(1)} %get-tuple-element.21.refs_0_), channel_id=1, source_target_pairs={{0,2},{1,3},{2,0},{3,1},{4,6},{5,7},{6,4},{7,5},{8,10},{9,11},{10,... | collective-permute-start | bytes 49160 | tf_op jit(solution)/shard_map/ppermute | solution.py:520
  11.7 5.2 %collective-permute-start.5 = (bf16[256,128]{1,0:T(8,128)(2,1)S(1)}, bf16[256,128]{1,0:T(8,128)(2,1)S(1)}, u32[]{:S(2)}, u32[]{:S(2)}) collective-permute-start(bf16[256,128]{1,0:T(8,128)(2,1)S(1)} %shard_map.131.refs_0_), channel_id=1, source_target_pairs={{0,17},{1,16},{2,19},{3,18},{4,21},{5,20},{6,23},{7,22},{8,25},{9,... | collective-permute-start | bytes 196616 | tf_op jit(solution)/shard_map/ppermute | solution.py:520
  14.2 4.3 %collective-permute-start.4 = (bf16[256,128]{1,0:T(8,128)(2,1)S(1)}, bf16[256,128]{1,0:T(8,128)(2,1)S(1)}, u32[]{:S(2)}, u32[]{:S(2)}) collective-permute-start(bf16[256,128]{1,0:T(8,128)(2,1)S(1)} %shard_map.131.refs_0_), channel_id=1, source_target_pairs={{0,16},{1,17},{2,18},{3,19},{4,20},{5,21},{6,22},{7,23},{8,24},{9,... | collective-permute-start | bytes 196616 | tf_op jit(solution)/shard_map/ppermute | solution.py:520
  14.8 4.3 %collective-permute-start.3 = (bf16[256,128]{1,0:T(8,128)(2,1)S(1)}, bf16[256,128]{1,0:T(8,128)(2,1)S(1)}, u32[]{:S(2)}, u32[]{:S(2)}) collective-permute-start(bf16[256,128]{1,0:T(8,128)(2,1)S(1)} %shard_map.131.refs_0_), channel_id=1, source_target_pairs={{0,1},{1,0},{2,3},{3,2},{4,5},{5,4},{6,7},{7,6},{8,9},{9,8},{10,11... | collective-permute-start | bytes 196616 | tf_op jit(solution)/shard_map/ppermute | solution.py:520
  15.3 5.0 %collective-permute-start.6 = (bf16[256,128]{1,0:T(8,128)(2,1)S(1)}, bf16[256,128]{1,0:T(8,128)(2,1)S(1)}, u32[]{:S(2)}, u32[]{:S(2)}) collective-permute-start(bf16[256,128]{1,0:T(8,128)(2,1)S(1)} %shard_map.131.refs_0_), channel_id=1, source_target_pairs={{0,8},{1,9},{2,10},{3,11},{4,12},{5,13},{6,14},{7,15},{8,0},{9,1},... | collective-permute-start | bytes 196616 | tf_op jit(solution)/shard_map/ppermute | solution.py:520
  16.9 3.4 %collective-permute-start.9 = (bf16[256,128]{1,0:T(8,128)(2,1)S(1)}, bf16[256,128]{1,0:T(8,128)(2,1)S(1)}, u32[]{:S(2)}, u32[]{:S(2)}) collective-permute-start(bf16[256,128]{1,0:T(8,128)(2,1)S(1)} %collective-permute-done.5.refs_3_), channel_id=1, source_target_pairs={{0,8},{1,9},{2,10},{3,11},{4,12},{5,13},{6,14},{7,15},{8,0},{9,1},... | collective-permute-start | bytes 196616 | tf_op jit(solution)/shard_map/ppermute | solution.py:520
  18.5 1.8 %collective-permute-start.8 = (bf16[256,128]{1,0:T(8,128)(2,1)S(1)}, bf16[256,128]{1,0:T(8,128)(2,1)S(1)}, u32[]{:S(2)}, u32[]{:S(2)}) collective-permute-start(bf16[256,128]{1,0:T(8,128)(2,1)S(1)} %collective-permute-done.4.refs_2_), channel_id=1, source_target_pairs={{0,8},{1,9},{2,10},{3,11},{4,12},{5,13},{6,14},{7,15},{8,0},{9,1},... | collective-permute-start | bytes 196616 | tf_op jit(solution)/shard_map/ppermute | solution.py:520
  19.0 1.3 %collective-permute-start.7 = (bf16[256,128]{1,0:T(8,128)(2,1)S(1)}, bf16[256,128]{1,0:T(8,128)(2,1)S(1)}, u32[]{:S(2)}, u32[]{:S(2)}) collective-permute-start(bf16[256,128]{1,0:T(8,128)(2,1)S(1)} %collective-permute-done.3.refs_1_), channel_id=1, source_target_pairs={{0,8},{1,9},{2,10},{3,11},{4,12},{5,13},{6,14},{7,15},{8,0},{9,1},... | collective-permute-start | bytes 196616 | tf_op jit(solution)/shard_map/ppermute | solution.py:520
  25.3 1.8 %collective-permute-start.10 = (bf16[1024,128]{1,0:T(8,128)(2,1)S(1)}, bf16[1024,128]{1,0:T(8,128)(2,1)S(1)}, u32[]{:S(2)}, u32[]{:S(2)}) collective-permute-start(bf16[1024,128]{1,0:T(8,128)(2,1)S(1)} %get-tuple-element.28.part_ref), channel_id=1, source_target_pairs={{0,8},{1,9},{2,10},{3,11},{4,12},{5,13},{6,14},{7,15},{8,0},{9,1},... | collective-permute-start | bytes 786440 | tf_op jit(solution)/shard_map/ppermute | solution.py:520
  25.9 1.3 %collective-permute-start.11 = (f32[136,128]{1,0:T(8,128)S(1)}, f32[136,128]{1,0:T(8,128)S(1)}, u32[]{:S(2)}, u32[]{:S(2)}) collective-permute-start(f32[136,128]{1,0:T(8,128)S(1)} %get-tuple-element.29.note_ref), channel_id=1, source_target_pairs={{0,8},{1,9},{2,10},{3,11},{4,12},{5,13},{6,14},{7,15},{8,0},{9,1},... | collective-permute-start | bytes 208904 | tf_op jit(solution)/shard_map/ppermute | solution.py:520

commit v5 on v4

--- a/solution.py
+++ b/solution.py
@@ -264,18 +264,20 @@
         for k in range(4):
             sender = place ^ (first_moves[k] ^ second_moves[n % 4] ^ n // 4 * core_move)
             at = k * 64
-            turned_ref[pl.ds(pl.multiple_of(sender * 32, 32), 32), :] = piece[at : at + 32, :].astype(f32)
+            turned = piece[at : at + 32, :].astype(f32)
+            for r in range(2):
+                turned_ref[pl.ds(r * 32 + sender, 16, stride=64), :] = turned[r * 16 : r * 16 + 16]
             plain_ref[pl.ds(pl.multiple_of(sender * 16, 16), 16), :] = piece[at + 32 : at + 48, :]
-            flat_ref[pl.ds(pl.multiple_of(sender * 16, 16), 16), :] = piece[at + 48 : at + 64, :].astype(f32)
+            flat = piece[at + 48 : at + 64, :].astype(f32)
+            flat_ref[pl.ds(sender, 1), :] = flat[0:1]
+            flat_ref[pl.ds(sender + 32, 1), :] = flat[1:2]
     for g in range(16):
-        for p in range(2):
-            groups_ref[p * 32 : p * 32 + 32, g * 128 : g * 128 + 128] = turned_ref[
-                pl.ds(p * 16 + g, 32, stride=32), :
-            ].astype(bf16)
+        groups_ref[:, g * 128 : g * 128 + 128] = turned_ref[g * 64 : g * 64 + 64, :].astype(bf16)
     for q in range(2):
         for g in range(8):
             at = (q * 8 + g) * 32
-            left_ref[at : at + 32, :] = turned_ref[pl.ds((core + q) % 2 * 16 + g, 32, stride=32), :].astype(bf16)
+            side = pl.multiple_of(g * 64 + (core + q) % 2 * 32, 32)
+            left_ref[at : at + 32, :] = turned_ref[pl.ds(side, 32), :].astype(bf16)
     source = lax.broadcasted_iota(jnp.int32, (128, 512), 0)
     target = lax.broadcasted_iota(jnp.int32, (128, 512), 1)
     copies = jnp.where(source == target // 128 * 32 + target % 32, 1.0 / 32.0, 0.0).astype(bf16)
@@ -317,12 +319,12 @@
     keep = second[0:32] // 8 == lax.broadcasted_iota(jnp.int32, (32, 512), 0) % 8
 
     def blocks(row):
-        placed = dot(flat_ref[pl.ds(row, 32, stride=16), :].astype(bf16), spread)
+        placed = dot(flat_ref[row * 32 : row * 32 + 32, :].astype(bf16), spread)
         return jnp.sum(jnp.where(keep, placed, 0.0).reshape(4, 8, 512), axis=1)
 
     labels = blocks(0).astype(jnp.int32)
     mask = blocks(1)
-    valid = jnp.sum(flat_ref[pl.ds(1, 32, stride=16), :], keepdims=True)
+    valid = jnp.sum(flat_ref[32:64, :], keepdims=True)
     factor = mask * (scale_ref[0] / valid)
     head2 = (2.0 * head_ref[...].astype(f32).T).astype(bf16)
     bins = lax.broadcasted_iota(jnp.int32, (64, 256), 0)
@@ -473,7 +475,7 @@
             pltpu.VMEM((512, 128), bf16),
             pltpu.VMEM((512, 128), bf16),
             pltpu.VMEM((512, 512), bf16),
-            pltpu.VMEM((512, 128), f32),
+            pltpu.VMEM((64, 128), f32),
             pltpu.VMEM((2048, 1024), bf16),
             pltpu.VMEM((2048, 128), f32),
             pltpu.VMEM((128, 2048), bf16),
@@ -496,19 +498,20 @@
     )(place, *others)
 
 
-def join_kernel(*refs):
+def join_kernel(after_ref, *refs):
+    del after_ref
     for n, part in enumerate(refs[:4]):
         refs[4][n * 64 : n * 64 + 64, :] = part[...]
 
 
-def join(parts):
+def join(parts, after):
     return pl.pallas_call(
         join_kernel,
         out_shape=jax.ShapeDtypeStruct((256, 128), bf16),
-        in_specs=[spec()] * 4,
+        in_specs=[spec(pl.ANY)] + [spec()] * 4,
         out_specs=spec(),
         compiler_params=limit(2),
-    )(*parts)
+    )(after, *parts)
 
 
 first_moves = (0, 2, 4, 6)
@@ -520,8 +523,8 @@
     return lax.ppermute(block, ("row", "col"), [(d, d ^ move) for d in range(32)])
 
 
-def gather(message):
-    line = join([message] + [swap(message, move) for move in first_moves[1:]])
+def gather(message, after):
+    line = join([message] + [swap(message, move) for move in first_moves[1:]], after)
     plane = [line] + [swap(line, move) for move in second_moves[1:]]
     return plane + [swap(block, core_move) for block in plane]
 
@@ -535,7 +538,7 @@
         pair_weight, pair_bias.reshape(1, 128), head_weight.T, head_bias.reshape(1, 64),
     )
     folded, by_left, by_right, bias = weights(pair, pair_bias, head_t, head_bias)
-    pieces = gather(message)
+    pieces = gather(message, bias)
     place = lax.axis_index(("row", "col")).astype(jnp.int32).reshape(1)
     part, note, groups = pairs(place, loss_scale.reshape(1), pieces, folded, bias, head_t)
     loss, align_grad, weight_grad = finish(

time: 29.3 us -> 29 us (0.990)
  transfers between devices with their start and end apart: 12 -> 12, of which waited for: 6 -> 7; matrix products, arithmetic and copies ran while one was open for 0% -> 0% of each run, Pallas kernels for 2% -> 2%
where the time goes in v5:
time: 29 us; the launch traced here: 28.8 us
  starting transfers between devices  9.89 us (34%)
  waiting for transfers between devices  8.86 us (31%)
  Pallas kernels  8.75 us (30%)
  between operations  1.34 us (5%)
    ppermute x12, starting transfers between devices, swap(): lax.ppermute(block, ('row', 'col'), [(d, d ^ move) for d in range(32)])  9.89 us
    ppermute x12, waiting for transfers between devices, swap(): lax.ppermute(block, ('row', 'col'), [(d, d ^ move) for d in range(32)])  8.86 us
    pallas_call x1, Pallas kernels, pairs(): pl.pallas_call(pairs_kernel, out_shape=(jax.ShapeDtypeStruct((1024, 128),...  4.88 us
    pallas_call x1, Pallas kernels, finish(): pl.pallas_call(finish_kernel, out_shape=(jax.ShapeDtypeStruct((1, 1), f32...  1.97 us
    pallas_call x1, Pallas kernels, prepare(): pl.pallas_call(prepare_kernel, out_shape=[jax.ShapeDtypeStruct((64, 128),...  1.31 us
    pallas_call x1, Pallas kernels, weights(): pl.pallas_call(weights_kernel, out_shape=(jax.ShapeDtypeStruct((1024, 128...  0.58 us
  transfers between devices with their start and end apart: 12, of which 7 were waited for; matrix products, arithmetic and copies ran while one was open for 0% of the time, Pallas kernels for 2%

profile of v5, /device:TPU:0, one launch (start us, length us, event | category | flops | bytes accessed | tf_op | source)
XLA Modules:
  0.0 28.8 jit_solution(9498630198843372438)
XLA Ops:
  0.6 1.3 %shard_map.130 = (bf16[64,128]{1,0:T(8,128)(2,1)S(1)}, bf16[32,2,256]{2,1,0:T(2,128)(2,1)S(1)}, f32[1,256]{1,0:T(1,128)S(1)}, bf16[64,256]{1,0:T(8,128)(2,1)S(1)...) custom-call(bf16[32,2,256]{2,1,0:T(2,128)(2,1)} %refs_0_.1, ...), custom_call_target="tpu_custom_call" | custom-call | tf_op jit(solution)/shard_map/pallas_call | solution.py:437
  2.0 5.1 %collective-permute-start.2 = (bf16[64,128]{1,0:T(8,128)(2,1)S(1)}, bf16[64,128]{1,0:T(8,128)(2,1)S(1)}, u32[]{:S(2)}, u32[]{:S(2)}) collective-permute-start(bf16[64,128]{1,0:T(8,128)(2,1)S(1)} %get-tuple-element.26.refs_0_), channel_id=1, source_target_pairs={{0,6},{1,7},{2,4},{3,5},{4,2},{5,3},{6,0},{7,1},{8,14},{9,15},{10,... | collective-permute-start | bytes 49160 | tf_op jit(solution)/shard_map/ppermute | solution.py:523
  7.1 0.0 collective-permute-start.1
  7.1 0.6 %collective-permute-start = (bf16[64,128]{1,0:T(8,128)(2,1)S(1)}, bf16[64,128]{1,0:T(8,128)(2,1)S(1)}, u32[]{:S(2)}, u32[]{:S(2)}) collective-permute-start(bf16[64,128]{1,0:T(8,128)(2,1)S(1)} %get-tuple-element.26.refs_0_), channel_id=1, source_target_pairs={{0,2},{1,3},{2,0},{3,1},{4,6},{5,7},{6,4},{7,5},{8,10},{9,11},{10,... | collective-permute-start | bytes 49160 | tf_op jit(solution)/shard_map/ppermute | solution.py:523
  7.7 0.6 %shard_map.131 = (bf16[1024,128]{1,0:T(8,128)(2,1)S(1)}, bf16[128,1024]{1,0:T(8,128)(2,1)S(1)}, bf16[128,1024]{1,0:T(8,128)(2,1)S(1)}, f32[64,1]{1,0:T(8,128)S(1)}) custom-call(bf16[1024,128]{1,0:T(8,128)(2,1)S(1)} %get-tuple-element.21.pair_ref, f32[1,128]{1,0:T(1,128)S(1)} %get-tuple-element.22.pair_bias_ref, ...), custom_call_target="tpu_custom_call" | custom-call | tf_op jit(solution)/shard_map/pallas_call | solution.py:448
  8.3 0.5 %collective-permute-done.2.refs_3_ = bf16[64,128]{1,0:T(8,128)(2,1)S(1)} collective-permute-done((bf16[64,128]{1,0:T(8,128)(2,1)S(1)}, bf16[64,128]{1,0:T(8,128)(2,1)S(1)}, u32[]{:S(2)}, u32[]{:S(2)}) %collective-permute-start.2) | collective-permute-done | bytes 16416 | tf_op jit(solution)/shard_map/ppermute | solution.py:523
  8.8 2.9 %collective-permute-done.1.refs_2_ = bf16[64,128]{1,0:T(8,128)(2,1)S(1)} collective-permute-done((bf16[64,128]{1,0:T(8,128)(2,1)S(1)}, bf16[64,128]{1,0:T(8,128)(2,1)S(1)}, u32[]{:S(2)}, u32[]{:S(2)}) %collective-permute-start.1) | collective-permute-done | bytes 16416 | tf_op jit(solution)/shard_map/ppermute | solution.py:523
  11.7 0.0 collective-permute-done.refs_1_
  11.7 2.5 %collective-permute-start.5 = (bf16[256,128]{1,0:T(8,128)(2,1)S(1)}, bf16[256,128]{1,0:T(8,128)(2,1)S(1)}, u32[]{:S(2)}, u32[]{:S(2)}) collective-permute-start(bf16[256,128]{1,0:T(8,128)(2,1)S(1)} %shard_map.132.refs_0_), channel_id=1, source_target_pairs={{0,17},{1,16},{2,19},{3,18},{4,21},{5,20},{6,23},{7,22},{8,25},{9,... | collective-permute-start | bytes 196616 | tf_op jit(solution)/shard_map/ppermute | solution.py:523
  14.2 0.5 %collective-permute-start.4 = (bf16[256,128]{1,0:T(8,128)(2,1)S(1)}, bf16[256,128]{1,0:T(8,128)(2,1)S(1)}, u32[]{:S(2)}, u32[]{:S(2)}) collective-permute-start(bf16[256,128]{1,0:T(8,128)(2,1)S(1)} %shard_map.132.refs_0_), channel_id=1, source_target_pairs={{0,16},{1,17},{2,18},{3,19},{4,20},{5,21},{6,22},{7,23},{8,24},{9,... | collective-permute-start | bytes 196616 | tf_op jit(solution)/shard_map/ppermute | solution.py:523
  14.8 0.5 %collective-permute-start.3 = (bf16[256,128]{1,0:T(8,128)(2,1)S(1)}, bf16[256,128]{1,0:T(8,128)(2,1)S(1)}, u32[]{:S(2)}, u32[]{:S(2)}) collective-permute-start(bf16[256,128]{1,0:T(8,128)(2,1)S(1)} %shard_map.132.refs_0_), channel_id=1, source_target_pairs={{0,1},{1,0},{2,3},{3,2},{4,5},{5,4},{6,7},{7,6},{8,9},{9,8},{10,11... | collective-permute-start | bytes 196616 | tf_op jit(solution)/shard_map/ppermute | solution.py:523
  15.3 0.0 collective-permute-start.6
  15.3 1.7 %collective-permute-done.5.refs_3_ = bf16[256,128]{1,0:T(8,128)(2,1)S(1)} collective-permute-done((bf16[256,128]{1,0:T(8,128)(2,1)S(1)}, bf16[256,128]{1,0:T(8,128)(2,1)S(1)}, u32[]{:S(2)}, u32[]{:S(2)}) %collective-permute-start.5) | collective-permute-done | bytes 65568 | tf_op jit(solution)/shard_map/ppermute | solution.py:523
  16.9 0.0 collective-permute-start.9
  17.0 1.5 %collective-permute-done.4.refs_2_ = bf16[256,128]{1,0:T(8,128)(2,1)S(1)} collective-permute-done((bf16[256,128]{1,0:T(8,128)(2,1)S(1)}, bf16[256,128]{1,0:T(8,128)(2,1)S(1)}, u32[]{:S(2)}, u32[]{:S(2)}) %collective-permute-start.4) | collective-permute-done | bytes 65568 | tf_op jit(solution)/shard_map/ppermute | solution.py:523
  18.5 0.0 collective-permute-start.8
  18.5 0.5 %collective-permute-done.3.refs_1_ = bf16[256,128]{1,0:T(8,128)(2,1)S(1)} collective-permute-done((bf16[256,128]{1,0:T(8,128)(2,1)S(1)}, bf16[256,128]{1,0:T(8,128)(2,1)S(1)}, u32[]{:S(2)}, u32[]{:S(2)}) %collective-permute-start.3) | collective-permute-done | bytes 65568 | tf_op jit(solution)/shard_map/ppermute | solution.py:523
  19.0 0.0 collective-permute-start.7
  19.7 0.0 collective-permute-done.6.refs_4_
  19.7 0.0 collective-permute-done.9.refs_7_
  19.7 0.0 collective-permute-done.8.refs_6_
  19.8 0.5 %collective-permute-done.7.refs_5_ = bf16[256,128]{1,0:T(8,128)(2,1)S(1)} collective-permute-done((bf16[256,128]{1,0:T(8,128)(2,1)S(1)}, bf16[256,128]{1,0:T(8,128)(2,1)S(1)}, u32[]{:S(2)}, u32[]{:S(2)}) %collective-permute-start.7) | collective-permute-done | bytes 65568 | tf_op jit(solution)/shard_map/ppermute | solution.py:523
  20.3 4.9 %shard_map.133 = (bf16[1024,128]{1,0:T(8,128)(2,1)S(1)}, f32[136,128]{1,0:T(8,128)S(1)}, bf16[64,2048]{1,0:T(8,128)(2,1)S(1)}) custom-call(s32[1]{0:T(128)} %bitcast.place_ref, f32[1]{0:T(128)} %bitcast.11.scale_ref, bf16[256,128]{1,0:T(8,128)(2,1)S(1)} %shard_map.132.refs_0_, bf16[256,128]{1,0:T(8,128)(2,1)S(1)} %collective-permute-done.3.refs_1_, ...), custom_call_target="tpu_custom_call" | custom-call | tf_op jit(solution)/shard_map/pallas_call | solution.py:464
  25.2 0.2 collective-permute-start.10
  25.4 0.4 %collective-permute-start.11 = (f32[136,128]{1,0:T(8,128)S(1)}, f32[136,128]{1,0:T(8,128)S(1)}, u32[]{:S(2)}, u32[]{:S(2)}) collective-permute-start(f32[136,128]{1,0:T(8,128)S(1)} %get-tuple-element.29.note_ref), channel_id=1, source_target_pairs={{0,8},{1,9},{2,10},{3,11},{4,12},{5,13},{6,14},{7,15},{8,0},{9,1},... | collective-permute-start | bytes 208904 | tf_op jit(solution)/shard_map/ppermute | solution.py:523
  25.7 1.1 %collective-permute-done.11.other_ref = f32[136,128]{1,0:T(8,128)S(1)} collective-permute-done((f32[136,128]{1,0:T(8,128)S(1)}, f32[136,128]{1,0:T(8,128)S(1)}, u32[]{:S(2)}, u32[]{:S(2)}) %collective-permute-start.11) | collective-permute-done | bytes 69664 | tf_op jit(solution)/shard_map/ppermute | solution.py:523
  26.9 0.0 collective-permute-done.10.other_part_ref
  26.9 2.0 %shard_map.134 = (f32[1,1]{1,0:T(1,128)}, f32[32,2,256]{2,1,0:T(2,128)}, f32[1024,128]{1,0:T(8,128)}) custom-call(s32[1]{0:T(128)} %bitcast.place_ref, bf16[1024,128]{1,0:T(8,128)(2,1)S(1)} %get-tuple-element.28.part_ref, bf16[1024,128]{1,0:T(8,128)(2,1)S(1)} %collective-permute-done.10.other_part_ref, f32[136,128]{1,0:T(8,128)S(1)} %get-tuple-element.29.note_ref, ...), custom_call_target="tpu_custom_call" | custom-call | tf_op jit(solution)/shard_map/pallas_call | solution.py:488
  (1 shorter events, 0.0 us)
Async XLA Ops:
  2.0 6.8 %collective-permute-start.2 = (bf16[64,128]{1,0:T(8,128)(2,1)S(1)}, bf16[64,128]{1,0:T(8,128)(2,1)S(1)}, u32[]{:S(2)}, u32[]{:S(2)}) collective-permute-start(bf16[64,128]{1,0:T(8,128)(2,1)S(1)} %get-tuple-element.26.refs_0_), channel_id=1, source_target_pairs={{0,6},{1,7},{2,4},{3,5},{4,2},{5,3},{6,0},{7,1},{8,14},{9,15},{10,... | collective-permute-start | bytes 49160 | tf_op jit(solution)/shard_map/ppermute | solution.py:523
  7.1 4.6 %collective-permute-start.1 = (bf16[64,128]{1,0:T(8,128)(2,1)S(1)}, bf16[64,128]{1,0:T(8,128)(2,1)S(1)}, u32[]{:S(2)}, u32[]{:S(2)}) collective-permute-start(bf16[64,128]{1,0:T(8,128)(2,1)S(1)} %get-tuple-element.26.refs_0_), channel_id=1, source_target_pairs={{0,4},{1,5},{2,6},{3,7},{4,0},{5,1},{6,2},{7,3},{8,12},{9,13},{10,... | collective-permute-start | bytes 49160 | tf_op jit(solution)/shard_map/ppermute | solution.py:523
  7.1 4.6 %collective-permute-start = (bf16[64,128]{1,0:T(8,128)(2,1)S(1)}, bf16[64,128]{1,0:T(8,128)(2,1)S(1)}, u32[]{:S(2)}, u32[]{:S(2)}) collective-permute-start(bf16[64,128]{1,0:T(8,128)(2,1)S(1)} %get-tuple-element.26.refs_0_), channel_id=1, source_target_pairs={{0,2},{1,3},{2,0},{3,1},{4,6},{5,7},{6,4},{7,5},{8,10},{9,11},{10,... | collective-permute-start | bytes 49160 | tf_op jit(solution)/shard_map/ppermute | solution.py:523
  11.7 5.2 %collective-permute-start.5 = (bf16[256,128]{1,0:T(8,128)(2,1)S(1)}, bf16[256,128]{1,0:T(8,128)(2,1)S(1)}, u32[]{:S(2)}, u32[]{:S(2)}) collective-permute-start(bf16[256,128]{1,0:T(8,128)(2,1)S(1)} %shard_map.132.refs_0_), channel_id=1, source_target_pairs={{0,17},{1,16},{2,19},{3,18},{4,21},{5,20},{6,23},{7,22},{8,25},{9,... | collective-permute-start | bytes 196616 | tf_op jit(solution)/shard_map/ppermute | solution.py:523
  14.2 4.3 %collective-permute-start.4 = (bf16[256,128]{1,0:T(8,128)(2,1)S(1)}, bf16[256,128]{1,0:T(8,128)(2,1)S(1)}, u32[]{:S(2)}, u32[]{:S(2)}) collective-permute-start(bf16[256,128]{1,0:T(8,128)(2,1)S(1)} %shard_map.132.refs_0_), channel_id=1, source_target_pairs={{0,16},{1,17},{2,18},{3,19},{4,20},{5,21},{6,22},{7,23},{8,24},{9,... | collective-permute-start | bytes 196616 | tf_op jit(solution)/shard_map/ppermute | solution.py:523
  14.8 4.3 %collective-permute-start.3 = (bf16[256,128]{1,0:T(8,128)(2,1)S(1)}, bf16[256,128]{1,0:T(8,128)(2,1)S(1)}, u32[]{:S(2)}, u32[]{:S(2)}) collective-permute-start(bf16[256,128]{1,0:T(8,128)(2,1)S(1)} %shard_map.132.refs_0_), channel_id=1, source_target_pairs={{0,1},{1,0},{2,3},{3,2},{4,5},{5,4},{6,7},{7,6},{8,9},{9,8},{10,11... | collective-permute-start | bytes 196616 | tf_op jit(solution)/shard_map/ppermute | solution.py:523
  15.3 4.4 %collective-permute-start.6 = (bf16[256,128]{1,0:T(8,128)(2,1)S(1)}, bf16[256,128]{1,0:T(8,128)(2,1)S(1)}, u32[]{:S(2)}, u32[]{:S(2)}) collective-permute-start(bf16[256,128]{1,0:T(8,128)(2,1)S(1)} %shard_map.132.refs_0_), channel_id=1, source_target_pairs={{0,8},{1,9},{2,10},{3,11},{4,12},{5,13},{6,14},{7,15},{8,0},{9,1},... | collective-permute-start | bytes 196616 | tf_op jit(solution)/shard_map/ppermute | solution.py:523
  16.9 2.8 %collective-permute-start.9 = (bf16[256,128]{1,0:T(8,128)(2,1)S(1)}, bf16[256,128]{1,0:T(8,128)(2,1)S(1)}, u32[]{:S(2)}, u32[]{:S(2)}) collective-permute-start(bf16[256,128]{1,0:T(8,128)(2,1)S(1)} %collective-permute-done.5.refs_3_), channel_id=1, source_target_pairs={{0,8},{1,9},{2,10},{3,11},{4,12},{5,13},{6,14},{7,15},{8,0},{9,1},... | collective-permute-start | bytes 196616 | tf_op jit(solution)/shard_map/ppermute | solution.py:523
  18.5 1.3 %collective-permute-start.8 = (bf16[256,128]{1,0:T(8,128)(2,1)S(1)}, bf16[256,128]{1,0:T(8,128)(2,1)S(1)}, u32[]{:S(2)}, u32[]{:S(2)}) collective-permute-start(bf16[256,128]{1,0:T(8,128)(2,1)S(1)} %collective-permute-done.4.refs_2_), channel_id=1, source_target_pairs={{0,8},{1,9},{2,10},{3,11},{4,12},{5,13},{6,14},{7,15},{8,0},{9,1},... | collective-permute-start | bytes 196616 | tf_op jit(solution)/shard_map/ppermute | solution.py:523
  19.0 1.3 %collective-permute-start.7 = (bf16[256,128]{1,0:T(8,128)(2,1)S(1)}, bf16[256,128]{1,0:T(8,128)(2,1)S(1)}, u32[]{:S(2)}, u32[]{:S(2)}) collective-permute-start(bf16[256,128]{1,0:T(8,128)(2,1)S(1)} %collective-permute-done.3.refs_1_), channel_id=1, source_target_pairs={{0,8},{1,9},{2,10},{3,11},{4,12},{5,13},{6,14},{7,15},{8,0},{9,1},... | collective-permute-start | bytes 196616 | tf_op jit(solution)/shard_map/ppermute | solution.py:523
  25.2 1.7 %collective-permute-start.10 = (bf16[1024,128]{1,0:T(8,128)(2,1)S(1)}, bf16[1024,128]{1,0:T(8,128)(2,1)S(1)}, u32[]{:S(2)}, u32[]{:S(2)}) collective-permute-start(bf16[1024,128]{1,0:T(8,128)(2,1)S(1)} %get-tuple-element.28.part_ref), channel_id=1, source_target_pairs={{0,8},{1,9},{2,10},{3,11},{4,12},{5,13},{6,14},{7,15},{8,0},{9,1},... | collective-permute-start | bytes 786440 | tf_op jit(solution)/shard_map/ppermute | solution.py:523
  25.4 1.5 %collective-permute-start.11 = (f32[136,128]{1,0:T(8,128)S(1)}, f32[136,128]{1,0:T(8,128)S(1)}, u32[]{:S(2)}, u32[]{:S(2)}) collective-permute-start(f32[136,128]{1,0:T(8,128)S(1)} %get-tuple-element.29.note_ref), channel_id=1, source_target_pairs={{0,8},{1,9},{2,10},{3,11},{4,12},{5,13},{6,14},{7,15},{8,0},{9,1},... | collective-permute-start | bytes 208904 | tf_op jit(solution)/shard_map/ppermute | solution.py:523
